TPU v7x, 256 devices: a whole 4x4x8 slice. The times are simulated.
256 devices in a mesh: var: 8 (over z), space: 32 (over x, y, core).
Axes of the slice: x: 4, y: 4, z: 8, core: 2. Of those that a mesh axis runs over, the one named last changes fastest.
Arguments:
- pixels: bfloat16 [96, 64, 4096], P('var', None, 'space'), may hold values from -6 to 6
- valid_mask: int32 [96], P('var'), may hold values from 0 to 1, as said below
- var_ids: int32 [96], P('var'), may hold values from 0 to 95, each once
- embed_weight: bfloat16 [96, 64, 1024], P('var'), may hold values from -0.75 to 0.75
- var_table: bfloat16 [96, 1024], replicated, may hold values from -3 to 3
- agg_query: float32 [1024], replicated, may hold values from -40 to 40
- agg_key: bfloat16 [1024, 1024], P('space'), may hold values from -0.1875 to 0.1875
- agg_value: bfloat16 [1024, 1024], replicated, may hold values from -0.1875 to 0.1875
- agg_out: bfloat16 [1024, 1024], replicated, may hold values from -0.1875 to 0.1875
- pos_embed: bfloat16 [4096, 1024], P('space'), may hold values from -3 to 3
- w_qkv: bfloat16 [1024, 3, 1024], P(None, None, 'var'), may hold values from -0.1875 to 0.1875
- w_out: bfloat16 [1024, 1024], P('var'), may hold values from -0.75 to 0.75
- w_up: bfloat16 [1024, 4096], P(None, 'var'), may hold values from -0.1875 to 0.1875
- w_down: bfloat16 [4096, 1024], P('var'), may hold values from -0.09375 to 0.09375
- cotangent: bfloat16 [4096, 1024], P('space'), may hold values from -6 to 6
Outputs:
- layer_out: bfloat16 [4096, 1024], P('space')
- grad_tokens: bfloat16 [4096, 1024], P('space')
- grad_qkv: float32 [1024, 3, 1024], P('space', None, 'var')
- grad_out: float32 [1024, 1024], P(('var', 'space'))
- grad_up: float32 [1024, 4096], P('space', 'var')
- grad_down: float32 [4096, 1024], P(('var', 'space'))
Inputs may be any that keep to these rules, and one draw needn't show every extreme that they name: `valid_mask`: exactly 5 entries are 0, the others 1.
All inputs are finite; a program needn't handle non-finite values.
Results may differ from a plain program's by a relative error of at most 0.02.
The roundings to bfloat16 on the way count: a program that leaves them out, or rounds other values in their place, can miss the bound.
Values may be sent and summed in bfloat16 or wider, within the bound.
A program may use at most 128 MiB of HBM per device.

v0:
```python
import jax
import jax.numpy as jnp
from jax import lax
from jax.sharding import PartitionSpec as P

D = 1024
H = 16
DH = 64


EPSILON = 1e-05
MASK_FLOOR = -1e30
HIGHEST = lax.Precision.HIGHEST


def matmul(left, right):
    return jnp.dot(left, right, preferred_element_type=jnp.float32)


def split_product(form, wide, narrow):
    high_part = wide.astype(jnp.bfloat16)
    low_part = (wide - lax.optimization_barrier(high_part).astype(jnp.float32)).astype(jnp.bfloat16)
    first = jnp.einsum(form, high_part, narrow, preferred_element_type=jnp.float32)
    return first + jnp.einsum(form, low_part, narrow, preferred_element_type=jnp.float32)


def layer_norm(inputs):
    values = inputs.astype(jnp.float32)
    centred = values - jnp.mean(values, -1, keepdims=True)
    spread = jnp.mean(centred * centred, -1, keepdims=True)
    return centred * lax.rsqrt(spread + EPSILON)


def norm_back(inputs, upstream):
    values = inputs.astype(jnp.float32)
    centred = values - jnp.mean(values, -1, keepdims=True)
    inv_std = lax.rsqrt(jnp.mean(centred * centred, -1, keepdims=True) + EPSILON)
    normed = centred * inv_std
    return inv_std * (
        upstream
        - jnp.mean(upstream, -1, keepdims=True)
        - normed * jnp.mean(upstream * normed, -1, keepdims=True)
    )


def gelu_back(pre_act, upstream):
    return jax.vjp(lambda inner: jax.nn.gelu(inner, approximate=False), pre_act)[1](upstream)[0]


def head_scores(left_rows, right_rows):
    return matmul(left_rows, right_rows.T) * DH ** (-0.5)


def head_forward(queries, key_rows, value_rows):
    scores = head_scores(queries, key_rows)
    row_max = jnp.max(scores, -1)
    exp_scores = jnp.exp(scores - row_max[:, None])
    row_sum = jnp.sum(exp_scores, -1)
    soft_probs = exp_scores / row_sum[:, None]
    context = matmul(soft_probs.astype(jnp.bfloat16), value_rows).astype(jnp.bfloat16)
    return (context, row_max, row_sum)


def query_backward(queries, key_rows, value_rows, row_max, row_sum, grad_context):
    scores = head_scores(queries, key_rows)
    soft_probs = jnp.exp(scores - row_max[:, None]) / row_sum[:, None]
    grad_probs = matmul(grad_context, value_rows.T)
    row_delta = jnp.sum(soft_probs * grad_probs, -1)
    grad_scores = (soft_probs * (grad_probs - row_delta[:, None]) * DH ** (-0.5)).astype(
        jnp.bfloat16
    )
    grad_key = matmul(grad_scores.T, queries)
    grad_value = matmul(soft_probs.astype(jnp.bfloat16).T, grad_context)
    return (matmul(grad_scores, key_rows), row_delta, grad_key, grad_value)


def split_heads(rows):
    return rows.reshape(rows.shape[0], rows.shape[1] // DH, DH).transpose(1, 0, 2)


def join_heads(stacked):
    return stacked.transpose(1, 0, 2).reshape(stacked.shape[1], stacked.shape[0] * DH)


def shards(
    pixels,
    valid_mask,
    var_ids,
    embed_weight,
    var_table,
    agg_query,
    agg_key,
    agg_value,
    agg_out,
    pos_embed,
    w_qkv,
    w_out,
    w_up,
    w_down,
    cotangent,
):
    raw_embed = jnp.einsum("vcp,vcd->vpd", pixels, embed_weight, preferred_element_type=jnp.float32)
    one_hot = (var_ids[:, None] == jnp.arange(var_table.shape[0], dtype=jnp.int32)[None, :]).astype(
        jnp.bfloat16
    )
    embedded = (raw_embed + matmul(one_hot, var_table)[:, None, :]).astype(jnp.bfloat16)
    key_part = jnp.einsum(
        "dhj,hj->dh",
        agg_key.astype(jnp.float32).reshape(agg_key.shape[0], H, DH),
        agg_query.reshape(H, DH),
        precision=HIGHEST,
    ).astype(jnp.bfloat16)
    key_dirs = lax.all_gather(key_part, "space", axis=0, tiled=True)
    arrived = lax.all_to_all(embedded, "var", split_axis=1, concat_axis=0, tiled=True)
    flag_rows = lax.all_gather(valid_mask, "var", axis=0, tiled=True)
    rows_here = arrived.shape[1]
    scores = jnp.einsum(
        "vpd,dh->vph", arrived, key_dirs, preferred_element_type=jnp.float32
    ) * DH ** (-0.5)
    mask_float = flag_rows.astype(jnp.float32)[:, None, None]
    floored = jnp.where(mask_float > 0, scores, MASK_FLOOR)
    weights = jnp.exp(floored - jnp.max(floored, 0)) * mask_float
    shares = weights / jnp.sum(weights, 0)
    pooled = split_product("vph,vpd->phd", shares, arrived)
    mixed_rows = (
        split_product("phd,dhj->phj", pooled, agg_value.reshape(D, H, DH))
        .reshape(rows_here, D)
        .astype(jnp.bfloat16)
    )
    pos_rows = lax.dynamic_slice_in_dim(pos_embed, lax.axis_index("var") * rows_here, rows_here, 0)
    token_part = (matmul(mixed_rows, agg_out) + pos_rows.astype(jnp.float32)).astype(jnp.bfloat16)
    tokens = lax.all_gather(token_part, "var", axis=0, tiled=True)
    normed_in = layer_norm(tokens).astype(jnp.bfloat16)
    qkv_local = jnp.einsum(
        "td,dcn->tcn", normed_in, w_qkv, preferred_element_type=jnp.float32
    ).astype(jnp.bfloat16)
    query_rows = qkv_local[:, 0]
    key_local = qkv_local[:, 1]
    value_local = qkv_local[:, 2]
    key_all, value_all = (
        lax.all_gather(key_local, "space", axis=0, tiled=True),
        lax.all_gather(value_local, "space", axis=0, tiled=True),
    )
    query_heads = split_heads(query_rows)
    key_heads = split_heads(key_all)
    value_heads = split_heads(value_all)
    context, row_max, row_sum = lax.map(
        lambda parts: head_forward(*parts), (query_heads, key_heads, value_heads)
    )
    context_rows = join_heads(context)
    attn_sum = lax.psum(matmul(context_rows, w_out), "var")
    middle = (tokens.astype(jnp.float32) + attn_sum).astype(jnp.bfloat16)
    normed_mid = layer_norm(middle).astype(jnp.bfloat16)
    pre_act = matmul(normed_mid, w_up)
    activated = jax.nn.gelu(pre_act, approximate=False).astype(jnp.bfloat16)
    down_sum = lax.psum(matmul(activated, w_down), "var")
    layer_out = (middle.astype(jnp.float32) + down_sum).astype(jnp.bfloat16)
    grad_down = matmul(activated.T, cotangent)
    grad_pre = gelu_back(pre_act, matmul(cotangent, w_down.T)).astype(jnp.bfloat16)
    grad_up = matmul(normed_mid.T, grad_pre)
    grad_mid_norm = lax.psum(matmul(grad_pre, w_up.T), "var")
    grad_middle = (cotangent.astype(jnp.float32) + norm_back(middle, grad_mid_norm)).astype(
        jnp.bfloat16
    )
    grad_out = matmul(context_rows.T, grad_middle)
    grad_context = matmul(grad_middle, w_out.T).astype(jnp.bfloat16)
    context_heads = split_heads(grad_context)
    grad_query, row_delta, grad_key, grad_value = lax.map(
        lambda parts: query_backward(*parts),
        (query_heads, key_heads, value_heads, row_max, row_sum, context_heads),
    )
    key_sum, value_sum = (
        lax.psum_scatter(join_heads(grad_key), "space", scatter_dimension=0, tiled=True),
        lax.psum_scatter(join_heads(grad_value), "space", scatter_dimension=0, tiled=True),
    )
    grad_qkv_rows = jnp.stack([join_heads(grad_query), key_sum, value_sum], 1).astype(jnp.bfloat16)
    grad_qkv = jnp.einsum(
        "td,tcn->dcn", normed_in, grad_qkv_rows, preferred_element_type=jnp.float32
    )
    grad_in = lax.psum(
        jnp.einsum("tcn,dcn->td", grad_qkv_rows, w_qkv, preferred_element_type=jnp.float32), "var"
    )
    grad_tokens = (grad_middle.astype(jnp.float32) + norm_back(tokens, grad_in)).astype(
        jnp.bfloat16
    )
    grad_qkv, grad_out, grad_up, grad_down = (
        lax.psum_scatter(grad_qkv, "space", scatter_dimension=0, tiled=True),
        lax.psum_scatter(grad_out, "space", scatter_dimension=0, tiled=True),
        lax.psum_scatter(grad_up, "space", scatter_dimension=0, tiled=True),
        lax.psum_scatter(grad_down, "space", scatter_dimension=0, tiled=True),
    )
    return (layer_out, grad_tokens, grad_qkv, grad_out, grad_up, grad_down)


def solution(mesh):
    in_specs = (
        P("var", None, "space"),
        P("var"),
        P("var"),
        P("var", None, None),
        P(),
        P(),
        P("space", None),
        P(),
        P(),
        P("space", None),
        P(None, None, "var"),
        P("var", None),
        P(None, "var"),
        P("var", None),
        P("space", None),
    )
    out_specs = (
        P("space", None),
        P("space", None),
        P("space", None, "var"),
        P(("var", "space"), None),
        P("space", "var"),
        P(("var", "space"), None),
    )
    return jax.shard_map(shards, mesh=mesh, in_specs=in_specs, out_specs=out_specs, check_vma=False)
```

profile of v0, /device:TPU:1, one launch (start us, length us, event | category | flops | bytes accessed | tf_op | source)
XLA Modules:
  0.0 1127.4 jit_solution(11762673066738014240)
XLA Ops:
  11.0 3.8 copy.78
  14.8 9.2 all-to-all-start
  25.5 95.4 %all-reduce = s32[96]{0:T(128)S(1)} all-reduce(s32[96]{0:T(128)S(1)} %dynamic-update-slice), channel_id=1, replica_groups=mesh['var'=8,'space'=32] {'var'}, use_global_device_ids=true, to_apply=%add | all-reduce | flops 96 | bytes 768
  121.5 27.2 %all-gather.2 = bf16[32,32,16]{1,2,0:T(8,128)(2,1)S(1)} all-gather(bf16[1,32,16]{1,2,0:T(8,128)(2,1)S(1)} %convert_bitcast_fusion.2), channel_id=1, replica_groups=mesh['var'=8,'space'=32] {'space'}, dimensions={0}, use_global_device_ids=true | all-gather | bytes 33792 | tf_op jit(solution)/shard_map/all_gather | solution.py:113
  149.0 4.0 copy.84
  154.2 4.0 copy.79
  161.4 5.3 fusion.41
  166.8 5.5 fusion.121
  175.3 20.8 %all_gather.17 = bf16[128,1024]{1,0:T(8,128)(2,1)S(1)} all-gather(bf16[16,1024]{1,0:T(8,128)(2,1)S(1)} %fusion.53), channel_id=1, replica_groups=mesh['var'=8,'space'=32] {'var'}, dimensions={0}, use_global_device_ids=true | all-gather | bytes 294912 | tf_op jit(solution)/shard_map/all_gather | solution.py:132
  198.5 50.0 %all-gather.6.cloned.1.call-done = bf16[4096,1,128]{0,2,1:T(8,128)(2,1)} async-done(((bf16[128,1,128]{0,2,1:T(8,128)(2,1)}), bf16[4096,1,128]{0,2,1:T(8,128)(2,1)}) %all-gather.6.cloned.1.call-update) | async-done | bytes 1048592 | tf_op jit(solution)/shard_map/all_gather | solution.py:141
  250.5 48.5 %all-gather.8.cloned.1.call-done = bf16[4096,1,128]{0,2,1:T(8,128)(2,1)} async-done(((bf16[128,1,128]{0,2,1:T(8,128)(2,1)}), bf16[4096,1,128]{0,2,1:T(8,128)(2,1)}) %all-gather.8.cloned.1.call-update) | async-done | bytes 1048592 | tf_op jit(solution)/shard_map/all_gather | solution.py:142
  299.0 2.7 copy.91
  301.7 4.8 while.28
  307.7 67.9 %all-reduce.8.cloned.1.call-done = f32[128,1024]{1,0:T(8,128)} async-done(((f32[128,1024]{1,0:T(8,128)}), f32[128,1024]{1,0:T(8,128)}) %all-reduce.8.cloned.1.call-update) | async-done | bytes 524304 | tf_op jit(solution)/shard_map/psum | solution.py:151
  382.5 71.9 %all-reduce.10.cloned.1.call-done = f32[128,1024]{1,0:T(8,128)} async-done(((f32[128,1024]{1,0:T(8,128)}), f32[128,1024]{1,0:T(8,128)}) %all-reduce.10.cloned.1.call-update) | async-done | bytes 524304 | tf_op jit(solution)/shard_map/psum | solution.py:161
  458.7 16.7 %while.29 = (s32[]{:T(128)}, bf16[2,128,64]{1,2,0:T(8,128)(2,1)}, f32[2,4096,64]{1,2,0:T(8,128)}, f32[2,4096,64]{1,2,0:T(8,128)}, bf16[2,128,64]{2,1,0:T(8,128)(...) while((s32[]{:T(128)}, bf16[2,128,64]{1,2,0:T(8,128)(2,1)}, ...), condition=%wide.region_17.18_spmd, body=%wide.region_15.17_spmd.sunk | while | flops 340787072 | bytes 54969680 | solution.py:168
  475.4 2.9 copy.94
  486.0 80.3 %reduce-scatter.8.cloned.1.call-done = f32[128,128]{1,0:T(8,128)} async-done(((f32[4096,128]{1,0:T(8,128)}), f32[128,128]{1,0:T(8,128)}) %reduce-scatter.8.cloned.1.call-update) | async-done | bytes 65552 | tf_op jit(solution)/shard_map/reduce_scatter | solution.py:174
  567.2 88.8 %reduce-scatter.6.cloned.1.call-done = f32[128,128]{1,0:T(8,128)} async-done(((f32[4096,128]{1,0:T(8,128)}), f32[128,128]{1,0:T(8,128)}) %reduce-scatter.6.cloned.1.call-update) | async-done | bytes 65552 | tf_op jit(solution)/shard_map/reduce_scatter | solution.py:173
  664.9 108.9 %all-reduce.12.cloned.1.call-done = f32[128,1024]{1,0:T(8,128)} async-done(((f32[128,1024]{1,0:T(8,128)}), f32[128,1024]{1,0:T(8,128)}) %all-reduce.12.cloned.1.call-update) | async-done | bytes 524304
  775.1 72.8 %all-reduce.14.cloned.1.call-done = (f32[128,1024]{1,0:T(8,128)}, f32[128,1024]{1,0:T(8,128)}) async-done(((f32[128,1024]{1,0:T(8,128)}, f32[128,1024]{1,0:T(8,128)}), (f32[128,1024]{1,0:T(8,128)}, f32[128,1024]{1,0:T(8,128)})) %all-reduce.14.cloned.1.call-update) | async-done | bytes 1048592 | tf_op jit(solution)/shard_map/psum | solution.py:156
  852.1 88.0 %reduce-scatter.12.cloned.1.call-done = f32[32,512]{1,0:T(8,128)} async-done(((f32[1024,512]{1,0:T(8,128)}), f32[32,512]{1,0:T(8,128)}) %reduce-scatter.12.cloned.1.call-update) | async-done | bytes 65552 | tf_op jit(solution)/shard_map/reduce_scatter | solution.py:189
  940.1 90.6 %reduce-scatter.14.cloned.1.call-done = f32[16,1024]{1,0:T(8,128)} async-done(((f32[512,1024]{1,0:T(8,128)}), f32[16,1024]{1,0:T(8,128)}) %reduce-scatter.14.cloned.1.call-update) | async-done | bytes 65552 | tf_op jit(solution)/shard_map/reduce_scatter | solution.py:190
  1030.7 90.2 %reduce-scatter.10.cloned.1.call-done = f32[32,3,128]{2,0,1:T(8,128)} async-done(((f32[1024,3,128]{2,0,1:T(8,128)}), f32[32,3,128]{2,0,1:T(8,128)}) %reduce-scatter.10.cloned.1.call-update) | async-done | bytes 49168 | tf_op jit(solution)/shard_map/reduce_scatter | solution.py:187
  (209 shorter events, 72.8 us)
Async XLA Ops:
  7.2 166.9 %copy-start = (bf16[1024,1024]{1,0:T(8,128)(2,1)S(1)}, bf16[1024,1024]{1,0:T(8,128)(2,1)}, u32[]{:S(2)}) copy-start(bf16[1024,1024]{1,0:T(8,128)(2,1)} %param.27) | copy-start | bytes 6291460
  14.8 10.5 copy-start.34
  14.8 106.2 %copy-start.25 = (bf16[32,1024]{1,0:T(8,128)(2,1)S(1)}, bf16[32,1024]{1,0:T(8,128)(2,1)}, u32[]{:S(2)}) copy-start(bf16[32,1024]{1,0:T(8,128)(2,1)} %param.25) | copy-start | bytes 196612
  14.8 106.3 %copy-start.33 = (f32[1024]{0:T(1024)S(1)}, f32[1024]{0:T(1024)}, u32[]{:S(2)}) copy-start(f32[1024]{0:T(1024)} %param.24) | copy-start | bytes 12292
  14.8 139.4 %all-to-all-start = ((bf16[12,128,1024]{2,0,1:T(8,128)(2,1)}), bf16[12,128,1024]{2,0,1:T(8,128)(2,1)}, u32[]{:S(2)}, u32[]{:S(2)}) async-start(bf16[12,128,1024]{2,0,1:T(8,128)(2,1)} %copy.78), calls=%async_computation | async-start | bytes 8388608 | tf_op jit(solution)/shard_map/all_to_all | solution.py:114
  24.0 224.5 %all-gather.6.cloned.1.call-start = ((), (), s32[]{:S(2)}) async-start(), calls=%async_computation.13 | async-start | bytes 1081344 | tf_op jit(solution)/shard_map/all_gather | solution.py:141
  173.7 22.7 %copy-start.8 = (bf16[1024,3,128]{0,2,1:T(8,128)(2,1)S(1)}, bf16[1024,3,128]{0,2,1:T(8,128)(2,1)}, u32[]{:S(2)}) copy-start(bf16[1024,3,128]{0,2,1:T(8,128)(2,1)} %copy.88) | copy-start | bytes 2359300
  197.6 101.4 %all-gather.8.cloned.1.call-start = ((), (), s32[]{:S(2)}) async-start(), calls=%async_computation.14 | async-start | bytes 1081344 | tf_op jit(solution)/shard_map/all_gather | solution.py:142
  198.3 177.3 %all-reduce.8.cloned.1.call-start = ((), (), s32[]{:S(2)}) async-start(), calls=%async_computation.6 | async-start | bytes 1048576 | tf_op jit(solution)/shard_map/psum | solution.py:151
  306.5 70.4 %copy-start.29 = (f32[2,128]{1,0:T(2,128)}, f32[2,128]{1,0:T(2,128)S(1)}, u32[]{:S(2)}) copy-start(f32[2,128]{1,0:T(2,128)S(1)} %get-tuple-element.313) | copy-start | bytes 3076
  306.5 72.2 %copy-start.23 = (bf16[2,128,64]{1,2,0:T(8,128)(2,1)}, bf16[2,128,64]{1,2,0:T(8,128)(2,1)S(1)}, u32[]{:S(2)}) copy-start(bf16[2,128,64]{1,2,0:T(8,128)(2,1)S(1)} %get-tuple-element.99) | copy-start | bytes 98308
  306.5 72.2 %copy-start.31 = (f32[2,128]{1,0:T(2,128)}, f32[2,128]{1,0:T(2,128)S(1)}, u32[]{:S(2)}) copy-start(f32[2,128]{1,0:T(2,128)S(1)} %get-tuple-element.314) | copy-start | bytes 3076
  306.5 72.2 %copy-start.15 = (bf16[128,1024]{1,0:T(8,128)(2,1)S(1)}, bf16[128,1024]{1,0:T(8,128)(2,1)}, u32[]{:S(2)}) copy-start(bf16[128,1024]{1,0:T(8,128)(2,1)} %param.33) | copy-start | bytes 786436
  307.6 146.8 %all-reduce.10.cloned.1.call-start = ((), (), s32[]{:S(2)}) async-start(), calls=%async_computation.7 | async-start | bytes 1048576 | tf_op jit(solution)/shard_map/psum | solution.py:161
  382.4 183.9 %reduce-scatter.8.cloned.1.call-start = ((), (), s32[]{:S(2)}) async-start(), calls=%async_computation.9 | async-start | bytes 2162688 | tf_op jit(solution)/shard_map/reduce_scatter | solution.py:174
  478.4 177.6 %reduce-scatter.6.cloned.1.call-start = ((), (), s32[]{:S(2)}) async-start(), calls=%async_computation.8 | async-start | bytes 2162688 | tf_op jit(solution)/shard_map/reduce_scatter | solution.py:173
  481.8 175.0 %copy-start.7 = (bf16[1024,3,128]{2,0,1:T(8,128)(2,1)S(1)}, bf16[1024,3,128]{2,0,1:T(8,128)(2,1)}, u32[]{:S(2)}) copy-start(bf16[1024,3,128]{2,0,1:T(8,128)(2,1)} %param.29) | copy-start | bytes 2359300
  481.8 292.0 %all-reduce.12.cloned.1.call-start = ((), (), s32[]{:S(2)}) async-start(), calls=%async_computation.15 | async-start | bytes 1048576
  484.8 173.3 %copy-start.22 = (bf16[128,512]{1,0:T(8,128)(2,1)S(1)}, bf16[128,512]{1,0:T(8,128)(2,1)}, u32[]{:S(2)}) copy-start(bf16[128,512]{1,0:T(8,128)(2,1)} %copy-done.21) | copy-start | bytes 393220
  486.0 361.9 %all-reduce.14.cloned.1.call-start = ((), (), s32[]{:S(2)}) async-start(), calls=%async_computation.16 | async-start | bytes 2097152 | tf_op jit(solution)/shard_map/psum | solution.py:156
  658.0 282.1 %reduce-scatter.12.cloned.1.call-start = ((), (), s32[]{:S(2)}) async-start(), calls=%async_computation.11 | async-start | bytes 2162688 | tf_op jit(solution)/shard_map/reduce_scatter | solution.py:189
  660.0 370.7 %reduce-scatter.14.cloned.1.call-start = ((), (), s32[]{:S(2)}) async-start(), calls=%async_computation.12 | async-start | bytes 2162688 | tf_op jit(solution)/shard_map/reduce_scatter | solution.py:190
  661.9 459.0 %reduce-scatter.10.cloned.1.call-start = ((), (), s32[]{:S(2)}) async-start(), calls=%async_computation.10 | async-start | bytes 1622016 | tf_op jit(solution)/shard_map/reduce_scatter | solution.py:187
  663.6 457.3 %copy-start.1 = (bf16[1024,1024]{1,0:T(8,128)(2,1)S(1)}, bf16[1024,1024]{1,0:T(8,128)(2,1)}, u32[]{:S(2)}) copy-start(bf16[1024,1024]{1,0:T(8,128)(2,1)} %param.27) | copy-start | bytes 6291460
  (34 other events, 77.6 us)
Sparse Core Ops, SparseCore 0:
  197.7 50.7 all-gather.5
  251.5 47.4 all-gather.7
  307.7 67.8 all-reduce.7
  382.5 71.8 all-reduce.9
  478.5 87.7 reduce-scatter.7
  570.0 85.8 reduce-scatter.5
  659.1 114.5 all-reduce.11
  776.3 71.6 all-reduce.13
  852.8 87.2 reduce-scatter.11
  944.9 85.8 reduce-scatter.13
  1035.6 85.2 reduce-scatter.9
where the time goes:
time: 1130 us
  waiting for transfers between devices  859 us (76%)
  blocking collectives  143 us (13%)
  matrix products  43.9 us (4%)
  local copies, waits for them, and re-layouts  42.5 us (4%)
  between operations  15.7 us (1%)
  other arithmetic  13.4 us (1%)
    unnamed x12, waiting for transfers between devices  110 us
    unnamed x1, blocking collectives  95.4 us
    reduce_scatter x1, waiting for transfers between devices, shards(): lax.psum_scatter(grad_down, 'space', scatter_dimension=0, tiled=True)  90.6 us
    reduce_scatter x1, waiting for transfers between devices, shards(): lax.psum_scatter(grad_qkv, 'space', scatter_dimension=0, tiled=True)  90.2 us
    reduce_scatter x1, waiting for transfers between devices, shards(): lax.psum_scatter(join_heads(grad_key), 'space', scatter_dimension=0, tile...  88.8 us
    reduce_scatter x1, waiting for transfers between devices, shards(): lax.psum_scatter(grad_up, 'space', scatter_dimension=0, tiled=True)  88 us
    reduce_scatter x1, waiting for transfers between devices, shards(): lax.psum_scatter(join_heads(grad_value), 'space', scatter_dimension=0, ti...  80.3 us
    psum x1, waiting for transfers between devices, shards(): down_sum = lax.psum(matmul(activated, w_down), 'var')  72.8 us
  transfers between devices with their start and end apart: 12, of which 11 were waited for; matrix products, arithmetic and copies ran while one was open for 3% of the time, Pallas kernels for 0%

commit v1 on v0

v1 whole, which is shorter than its diff:
```python
import functools
import jax
import jax.numpy as jnp
from jax import lax
from jax.experimental import pallas as pl
from jax.experimental.pallas import tpu as pltpu
from jax.sharding import PartitionSpec as P

D = 1024
H = 16
DH = 64
EPSILON = 1e-05
MASK_FLOOR = -1e30
HIGHEST = lax.Precision.HIGHEST
MESH = pl.DeviceIdType.MESH
VMEM = pl.BlockSpec(memory_space=pltpu.VMEM)


def matmul(left, right):
    return jnp.dot(left, right, preferred_element_type=jnp.float32)


def transfer_kernel(axis, n, count, spread, *refs):
    ins, outs = refs[:count], refs[count : 2 * count]
    lands = refs[2 * count : 3 * count]
    send_sem, recv_sem = refs[3 * count :]
    me = lax.axis_index(axis)
    barrier = pltpu.get_barrier_semaphore()

    def greet(d, carry):
        pl.semaphore_signal(
            barrier, inc=1, device_id={axis: lax.rem(me + d, n)}, device_id_type=MESH
        )
        return carry

    lax.fori_loop(1, n, greet, 0)
    pl.semaphore_wait(barrier, n - 1)

    def send(d, carry):
        there = lax.rem(me + d, n)
        for k in range(count):
            pltpu.make_async_remote_copy(
                src_ref=ins[k].at[there] if spread else ins[k],
                dst_ref=lands[k].at[d - 1],
                send_sem=send_sem.at[k],
                recv_sem=recv_sem.at[k],
                device_id={axis: there},
                device_id_type=MESH,
            ).start()
        return carry

    lax.fori_loop(1, n, send, 0)
    for k in range(count):
        outs[k][me] = ins[k][me] if spread else ins[k][...]
    for k in range(count):
        pltpu.make_async_copy(lands[k], lands[k], recv_sem.at[k]).wait()

    def place(d, carry):
        for k in range(count):
            outs[k][lax.rem(me - d + n, n)] = lands[k][d - 1]
        return carry

    lax.fori_loop(1, n, place, 0)
    for k in range(count):
        pltpu.make_async_copy(lands[k], lands[k], send_sem.at[k]).wait()


def transfer(axis, n, number, spread, *arrays):
    blocks = [a.shape[1:] if spread else a.shape for a in arrays]
    count = len(arrays)
    return pl.pallas_call(
        functools.partial(transfer_kernel, axis, n, count, spread),
        out_shape=[
            jax.ShapeDtypeStruct((n,) + b, a.dtype) for a, b in zip(arrays, blocks)
        ],
        in_specs=[VMEM] * count,
        out_specs=[VMEM] * count,
        scratch_shapes=[pltpu.VMEM((n - 1,) + b, a.dtype) for a, b in zip(arrays, blocks)]
        + [pltpu.SemaphoreType.DMA((count,)), pltpu.SemaphoreType.DMA((count,))],
        compiler_params=pltpu.CompilerParams(
            collective_id=number, has_side_effects=True, vmem_limit_bytes=48 * 2**20
        ),
        name="transfer_%d" % number,
    )(*arrays)


def gather(axis, n, number, *arrays):
    return transfer(axis, n, number, False, *arrays)


def exchange(axis, n, number, *arrays):
    return transfer(axis, n, number, True, *arrays)


def layer_norm(inputs):
    values = inputs.astype(jnp.float32)
    centred = values - jnp.mean(values, -1, keepdims=True)
    spread = jnp.mean(centred * centred, -1, keepdims=True)
    return centred * lax.rsqrt(spread + EPSILON)


def norm_back(inputs, upstream):
    values = inputs.astype(jnp.float32)
    centred = values - jnp.mean(values, -1, keepdims=True)
    inv_std = lax.rsqrt(jnp.mean(centred * centred, -1, keepdims=True) + EPSILON)
    normed = centred * inv_std
    return inv_std * (
        upstream
        - jnp.mean(upstream, -1, keepdims=True)
        - normed * jnp.mean(upstream * normed, -1, keepdims=True)
    )


def gelu_back(pre_act, upstream):
    return jax.vjp(lambda inner: jax.nn.gelu(inner, approximate=False), pre_act)[1](upstream)[0]


def shards(nvar, nspace, pixels, valid_mask, var_ids, embed_weight, var_table, agg_query, agg_key,
           agg_value, agg_out, pos_embed, w_qkv, w_out, w_up, w_down, cotangent):
    bf16, f32 = jnp.bfloat16, jnp.float32
    at = lax.axis_index("var")
    slots, rows = pixels.shape[0], pixels.shape[2]
    part = rows // nvar
    key_part = jnp.einsum(
        "dhj,hj->dh", agg_key.astype(f32).reshape(agg_key.shape[0], H, DH),
        agg_query.reshape(H, DH), precision=HIGHEST).astype(bf16)
    key_dirs, = gather("space", nspace, 0, jnp.pad(key_part, ((0, 0), (0, 128 - H))))
    key_dirs = key_dirs.reshape(D, 128)[:, :H]
    raw_embed = jnp.einsum("vcp,vcd->vpd", pixels, embed_weight, preferred_element_type=f32)
    one_hot = (var_ids[:, None] == jnp.arange(var_table.shape[0], dtype=jnp.int32)[None, :]).astype(bf16)
    embedded = (raw_embed + matmul(one_hot, var_table)[:, None, :]).astype(bf16)
    scores = jnp.einsum("vpd,dh->vph", embedded, key_dirs, preferred_element_type=f32) * DH ** (-0.5)
    mask = valid_mask.astype(f32)[:, None, None]
    floored = jnp.where(mask > 0, scores, MASK_FLOOR)
    top = jnp.max(floored, 0)
    weights = jnp.exp(floored - top) * mask
    total = jnp.sum(weights, 0)
    shares = weights / total
    level = top + jnp.log(total)
    values = jnp.einsum("vpd,de->vpe", embedded, agg_value, preferred_element_type=f32)
    pooled = jnp.sum(jnp.repeat(shares, DH, axis=2) * values, 0)
    pieces, levels = exchange(
        "var", nvar, 1, pooled.astype(bf16).reshape(nvar, part, D),
        jnp.pad(level, ((0, 0), (0, 128 - H))).reshape(nvar, part, 128))
    levels = levels[:, :, :H]
    lifts = jnp.exp(levels - jnp.max(levels, 0))
    lifts = lifts / jnp.sum(lifts, 0)
    mixed = jnp.sum(jnp.repeat(lifts, DH, axis=2) * pieces.astype(f32), 0).astype(bf16)
    pos_rows = lax.dynamic_slice_in_dim(pos_embed, at * part, part, 0)
    token_part = (matmul(mixed, agg_out) + pos_rows.astype(f32)).astype(bf16)
    tokens, = gather("var", nvar, 2, token_part)
    tokens = tokens.reshape(rows, D)
    normed_in = layer_norm(tokens).astype(bf16)
    qkv = jnp.einsum("td,dcn->tcn", normed_in, w_qkv, preferred_element_type=f32).astype(bf16)
    queries = qkv[:, 0]
    keys, vals = gather("space", nspace, 3, qkv[:, 1], qkv[:, 2])
    keys = keys.reshape(nspace * rows, 128)
    vals = vals.reshape(nspace * rows, 128)
    heads = [slice(0, 64), slice(64, 128)]
    kept, contexts = [], []
    for h in heads:
        scores_t = lax.dot_general(keys[:, h], queries[:, h], (((1,), (1,)), ((), ())),
                                   preferred_element_type=f32) * DH ** (-0.5)
        exps = jnp.exp(scores_t - jnp.max(scores_t, 0))
        probs = exps / jnp.sum(exps, 0)
        kept.append(probs)
        contexts.append(lax.dot_general(probs.astype(bf16), vals[:, h], (((0,), (0,)), ((), ())),
                                        preferred_element_type=f32).astype(bf16))
    context = jnp.concatenate(contexts, 1)

    def reduce_rows(partial, number):
        arrived, = exchange("var", nvar, number, partial.astype(bf16).reshape(nvar, part, D))
        return jnp.sum(arrived.astype(f32), 0)

    def own(array):
        return lax.dynamic_slice_in_dim(array, at * part, part, 0)

    middle_part = (own(tokens).astype(f32) + reduce_rows(matmul(context, w_out), 4)).astype(bf16)
    middle, = gather("var", nvar, 5, middle_part)
    middle = middle.reshape(rows, D)
    normed_mid = layer_norm(middle).astype(bf16)
    pre_act = matmul(normed_mid, w_up)
    activated = jax.nn.gelu(pre_act, approximate=False).astype(bf16)
    layer_part = (middle_part.astype(f32) + reduce_rows(matmul(activated, w_down), 6)).astype(bf16)
    layer_out, = gather("var", nvar, 7, layer_part)
    layer_out = layer_out.reshape(rows, D)
    grad_down = matmul(activated.T, cotangent)
    grad_pre = gelu_back(pre_act, matmul(cotangent, w_down.T)).astype(bf16)
    grad_up = matmul(normed_mid.T, grad_pre)
    grad_mid_norm = reduce_rows(matmul(grad_pre, w_up.T), 8)
    grad_mid_part = (own(cotangent).astype(f32) + norm_back(middle_part, grad_mid_norm)).astype(bf16)
    grad_middle, = gather("var", nvar, 9, grad_mid_part)
    grad_middle = grad_middle.reshape(rows, D)
    grad_out = matmul(context.T, grad_middle)
    grad_context = matmul(grad_middle, w_out.T).astype(bf16)
    grad_q, grad_k, grad_v = [], [], []
    for h, probs in zip(heads, kept):
        upstream = grad_context[:, h]
        grad_probs = lax.dot_general(vals[:, h], upstream, (((1,), (1,)), ((), ())),
                                     preferred_element_type=f32)
        delta = jnp.sum(probs * grad_probs, 0)
        grad_scores = (probs * (grad_probs - delta) * DH ** (-0.5)).astype(bf16)
        grad_q.append(lax.dot_general(grad_scores, keys[:, h], (((0,), (0,)), ((), ())),
                                      preferred_element_type=f32))
        grad_k.append(matmul(grad_scores, queries[:, h]))
        grad_v.append(matmul(probs.astype(bf16), upstream))
    shape = (nspace, rows, 128)
    k_parts, v_parts = exchange(
        "space", nspace, 10, jnp.concatenate(grad_k, 1).astype(bf16).reshape(shape),
        jnp.concatenate(grad_v, 1).astype(bf16).reshape(shape))
    grad_rows = jnp.concatenate(
        [jnp.concatenate(grad_q, 1).astype(bf16), jnp.sum(k_parts.astype(f32), 0).astype(bf16),
         jnp.sum(v_parts.astype(f32), 0).astype(bf16)], 1)
    grad_qkv = matmul(normed_in.T, grad_rows)
    grad_in = reduce_rows(lax.dot_general(grad_rows, w_qkv.reshape(D, 384), (((1,), (1,)), ((), ())),
                                          preferred_element_type=f32), 11)
    grad_tok_part = (grad_mid_part.astype(f32) + norm_back(own(tokens), grad_in)).astype(bf16)
    grad_tokens, = gather("var", nvar, 12, grad_tok_part)
    sums = []
    for number, grad in ((13, grad_qkv), (14, grad_out), (15, grad_up), (16, grad_down)):
        shape = (nspace, grad.shape[0] // nspace, grad.shape[1])
        if shape[1] < 16:
            shape = (nspace, 16, grad.shape[0] * grad.shape[1] // nspace // 16)
        arrived, = exchange("space", nspace, number, grad.astype(bf16).reshape(shape))
        sums.append(jnp.sum(arrived.astype(f32), 0).reshape(grad.shape[0] // nspace, grad.shape[1]))
    return (layer_out, grad_tokens.reshape(rows, D), sums[0].reshape(D // nspace, 3, 128),
            sums[1], sums[2], sums[3])


def solution(mesh):
    in_specs = (
        P("var", None, "space"), P("var"), P("var"), P("var", None, None), P(), P(),
        P("space", None), P(), P(), P("space", None), P(None, None, "var"), P("var", None),
        P(None, "var"), P("var", None), P("space", None),
    )
    out_specs = (
        P("space", None), P("space", None), P("space", None, "var"),
        P(("var", "space"), None), P("space", "var"), P(("var", "space"), None),
    )
    body = functools.partial(shards, mesh.shape["var"], mesh.shape["space"])
    return jax.shard_map(body, mesh=mesh, in_specs=in_specs, out_specs=out_specs, check_vma=False)
```

time: 1130 us -> 392 us (0.35)
  waiting for transfers between devices: 859 us -> 0 us
  Pallas kernels: 0 us -> 291 us
  blocking collectives: 143 us -> 0 us
  between operations: 15.7 us -> 1.6 us
    reduce_scatter x5 -> x0, waiting for transfers between devices: 438 us -> none  [the longest x1 90.6 us: shards(): lax.psum_scatter(grad_down, 'space', scatter_dimension=0, tiled=True)]
    pallas_call x0 -> x17, Pallas kernels: none -> 291 us  [transfer(): pl.pallas_call(functools.partial(transfer_kernel, axis, n, count, spread)...]
    psum x3 -> x0, waiting for transfers between devices: 213 us -> none  [the longest x1 72.8 us: shards(): down_sum = lax.psum(matmul(activated, w_down), 'var')]
    unnamed x12 -> x0, waiting for transfers between devices: 110 us -> none
    all_gather x2 -> x0, waiting for transfers between devices: 98.4 us -> none  [the longest x1 50 us: shards(): lax.all_gather(key_local, 'space', axis=0, tiled=True)]
    unnamed x1 -> x0, blocking collectives: 95.4 us -> none
    all_gather x2 -> x0, blocking collectives: 48 us -> none  [the longest x1 27.2 us: shards(): key_dirs = lax.all_gather(key_part, 'space', axis=0, tiled=True)]
    dot_general x25 -> x16, matrix products: 24.6 us -> 18.5 us  [matmul(): return jnp.dot(left, right, preferred_element_type=jnp.float32)]
  transfers between devices with their start and end apart: 12 -> 0, of which waited for: 11 -> 0; matrix products, arithmetic and copies ran while one was open for 3% -> 0% of each run, Pallas kernels for 0% -> 0%
where the time goes in v1:
time: 392 us; the launch traced here: 388 us
  Pallas kernels  291 us (74%)
  matrix products  44.2 us (11%)
  local copies, waits for them, and re-layouts  34 us (9%)
  other arithmetic  17.2 us (4%)
    pallas_call x17, Pallas kernels, transfer(): pl.pallas_call(functools.partial(transfer_kernel, axis, n, count, spread)...  291 us
    dot_general x16, matrix products, matmul(): return jnp.dot(left, right, preferred_element_type=jnp.float32)  18.5 us
    unnamed x101, local copies, waits for them, and re-layouts  10.5 us
    another operation x6, local copies, waits for them, and re-layouts  8.3 us

profile of v1, /device:TPU:1, one launch (start us, length us, event | category | flops | bytes accessed | tf_op | source)
XLA Modules:
  0.0 388.4 jit_solution(2243456890028881959)
XLA Ops:
  2.0 4.3 %add_convert_fusion = bf16[12,128,1024]{2,1,0:T(8,128)(2,1)} fusion(f32[12,1024]{1,0:T(8,128)S(1)} %fusion.69, bf16[12,64,128]{2,1,0:T(8,128)(2,1)} %param.15, bf16[12,64,1024]{2,1,0:T(8,128)(2,1)} %param.18), kind=kOutput, calls=%fused_computation.1 | convolution fusion | flops 204472320 | bytes 4964352 | tf_op jit(solution)/shard_map/vcp,vcd->vpd/dot_general | solution.py:129
  6.9 12.5 %transfer_0.1 = bf16[32,32,128]{2,1,0:T(8,128)(2,1)S(1)} custom-call(bf16[32,128]{1,0:T(8,128)(2,1)S(1)} %pad.8.refs_0_), custom_call_target="tpu_custom_call" | custom-call | tf_op jit(solution)/shard_map/transfer_0/pallas_call | solution.py:71
  19.4 2.8 fusion.81
  22.4 3.1 broadcast_in_dim.18
  25.5 6.6 %copy.48 = f32[12,128,1024]{2,1,0:T(8,128)} copy(f32[12,128,1024]{1,2,0:T(8,128)} %bitcast.118) | data formatting | bytes 12582912 | tf_op jit(solution)/shard_map/reshape | solution.py:141
  32.1 6.6 %multiply_reduce_fusion = bf16[128,1024]{1,0:T(8,128)(2,1)S(1)} fusion(f32[12,128,1024]{2,1,0:T(8,128)} %copy.48, bf16[12,128,1024]{2,1,0:T(8,128)(2,1)} %add_convert_fusion, bf16[1024,1024]{1,0:T(8,128)(2,1)S(1)} %copy-done), kind=kOutput, calls=%fused_computation | convolution fusion | flops 3224240128 | bytes 11796480 | tf_op jit(solution)/shard_map/vpd,de->vpe/dot_general | solution.py:140
  38.8 15.5 %transfer_1.1 = (bf16[8,16,1024]{2,1,0:T(8,128)(2,1)S(1)}, f32[8,16,128]{2,1,0:T(8,128)S(1)}) custom-call(bf16[8,16,1024]{2,1,0:T(8,128)(2,1)S(1)} %bitcast.112, f32[8,16,128]{2,1,0:T(8,128)S(1)} %bitcast.113), custom_call_target="tpu_custom_call" | custom-call | tf_op jit(solution)/shard_map/transfer_1/pallas_call | solution.py:71
  58.9 8.1 %transfer_2.1 = bf16[8,16,1024]{2,1,0:T(8,128)(2,1)S(1)} custom-call(bf16[16,1024]{1,0:T(8,128)(2,1)S(1)} %fusion.6.refs_0_), custom_call_target="tpu_custom_call" | custom-call | tf_op jit(solution)/shard_map/transfer_2/pallas_call | solution.py:71
  71.4 43.0 %transfer_3.1 = (bf16[32,128,128]{2,1,0:T(8,128)(2,1)S(1)}, bf16[32,128,128]{2,1,0:T(8,128)(2,1)S(1)}) custom-call(bf16[128,128]{1,0:T(8,128)(2,1)S(1)} %get-tuple-element.41.refs_0_, bf16[128,128]{1,0:T(8,128)(2,1)S(1)} %get-tuple-element.40.refs_1_), custom_call_target="tpu_custom_call" | custom-call | tf_op jit(solution)/shard_map/transfer_3/pallas_call | solution.py:71
  119.5 9.9 %transfer_4.1 = bf16[8,16,1024]{2,1,0:T(8,128)(2,1)S(1)} custom-call(bf16[8,16,1024]{2,1,0:T(8,128)(2,1)S(1)} %bitcast.108), custom_call_target="tpu_custom_call" | custom-call | tf_op jit(solution)/shard_map/transfer_4/pallas_call | solution.py:71
  130.3 10.0 %transfer_5.1 = bf16[8,16,1024]{2,1,0:T(8,128)(2,1)S(1)} custom-call(bf16[16,1024]{1,0:T(8,128)(2,1)S(1)} %get-tuple-element.35.refs_0_), custom_call_target="tpu_custom_call" | custom-call | tf_op jit(solution)/shard_map/transfer_5/pallas_call | solution.py:71
  145.7 29.5 %transfer_15.1 = bf16[32,32,512]{2,1,0:T(8,128)(2,1)S(1)} custom-call(bf16[32,32,512]{2,1,0:T(8,128)(2,1)S(1)} %bitcast.100), custom_call_target="tpu_custom_call" | custom-call | tf_op jit(solution)/shard_map/transfer_15/pallas_call | solution.py:71
  177.1 11.4 %transfer_6.1 = bf16[8,16,1024]{2,1,0:T(8,128)(2,1)S(1)} custom-call(bf16[8,16,1024]{2,1,0:T(8,128)(2,1)S(1)} %bitcast.111), custom_call_target="tpu_custom_call" | custom-call | tf_op jit(solution)/shard_map/transfer_6/pallas_call | solution.py:71
  189.0 9.6 %transfer_8.1 = bf16[8,16,1024]{2,1,0:T(8,128)(2,1)S(1)} custom-call(bf16[8,16,1024]{2,1,0:T(8,128)(2,1)S(1)} %bitcast.110), custom_call_target="tpu_custom_call" | custom-call | tf_op jit(solution)/shard_map/transfer_8/pallas_call | solution.py:71
  199.2 12.1 %transfer_9.1 = bf16[8,16,1024]{2,1,0:T(8,128)(2,1)S(1)} custom-call(bf16[16,1024]{1,0:T(8,128)(2,1)S(1)} %get-tuple-element.42.refs_0_), custom_call_target="tpu_custom_call" | custom-call | tf_op jit(solution)/shard_map/transfer_9/pallas_call | solution.py:71
  215.7 14.3 %transfer_14.1 = bf16[32,16,256]{2,1,0:T(8,128)(2,1)S(1)} custom-call(bf16[32,16,256]{2,1,0:T(8,128)(2,1)S(1)} %copy-done.5), custom_call_target="tpu_custom_call" | custom-call | tf_op jit(solution)/shard_map/transfer_14/pallas_call | solution.py:71
  232.0 2.8 multiply_reduce_fusion.2
  237.1 2.8 multiply_reduce_fusion.1
  263.2 39.4 %transfer_10.1 = (bf16[32,128,128]{2,1,0:T(8,128)(2,1)S(1)}, bf16[32,128,128]{2,1,0:T(8,128)(2,1)S(1)}) custom-call(bf16[32,128,128]{2,1,0:T(8,128)(2,1)S(1)} %pad_maximum_fusion.refs_0_, bf16[32,128,128]{2,1,0:T(8,128)(2,1)S(1)} %pad_maximum_fusion.1.refs_1_), custom_call_target="tpu_custom_call" | custom-call | tf_op jit(solution)/shard_map/transfer_10/pallas_call | solution.py:71
  307.9 20.8 %transfer_13.1 = bf16[32,32,384]{2,1,0:T(8,128)(2,1)S(1)} custom-call(bf16[32,32,384]{2,1,0:T(8,128)(2,1)S(1)} %bitcast.102), custom_call_target="tpu_custom_call" | custom-call | tf_op jit(solution)/shard_map/transfer_13/pallas_call | solution.py:71
  329.9 12.0 %transfer_11.1 = bf16[8,16,1024]{2,1,0:T(8,128)(2,1)S(1)} custom-call(bf16[8,16,1024]{2,1,0:T(8,128)(2,1)S(1)} %bitcast.109), custom_call_target="tpu_custom_call" | custom-call | tf_op jit(solution)/shard_map/transfer_11/pallas_call | solution.py:71
  342.4 9.6 %transfer_12.1 = bf16[8,16,1024]{2,1,0:T(8,128)(2,1)S(1)} custom-call(bf16[16,1024]{1,0:T(8,128)(2,1)S(1)} %fusion.47.refs_0_), custom_call_target="tpu_custom_call" | custom-call | tf_op jit(solution)/shard_map/transfer_12/pallas_call | solution.py:71
  352.5 22.6 %transfer_16.1 = bf16[32,16,1024]{2,1,0:T(8,128)(2,1)S(1)} custom-call(bf16[32,16,1024]{2,1,0:T(8,128)(2,1)S(1)} %bitcast.101), custom_call_target="tpu_custom_call" | custom-call | tf_op jit(solution)/shard_map/transfer_16/pallas_call | solution.py:71
  375.8 11.2 %transfer_7.1 = bf16[8,16,1024]{2,1,0:T(8,128)(2,1)S(1)} custom-call(bf16[16,1024]{1,0:T(8,128)(2,1)S(1)} %get-tuple-element.43.refs_0_), custom_call_target="tpu_custom_call" | custom-call | tf_op jit(solution)/shard_map/transfer_7/pallas_call | solution.py:71
  (197 shorter events, 66.5 us)
Async XLA Ops:
  0.6 31.5 %copy-start = (bf16[1024,1024]{1,0:T(8,128)(2,1)S(1)}, bf16[1024,1024]{1,0:T(8,128)(2,1)}, u32[]{:S(2)}) copy-start(bf16[1024,1024]{1,0:T(8,128)(2,1)} %param.22) | copy-start | bytes 6291460
  1.9 4.3 %copy-start.26 = (bf16[32,1024]{1,0:T(8,128)(2,1)S(1)}, bf16[32,1024]{1,0:T(8,128)(2,1)}, u32[]{:S(2)}) copy-start(bf16[32,1024]{1,0:T(8,128)(2,1)} %param.21) | copy-start | bytes 196612
  1.9 4.4 %copy-start.39 = (f32[1024]{0:T(1024)S(1)}, f32[1024]{0:T(1024)}, u32[]{:S(2)}) copy-start(f32[1024]{0:T(1024)} %param.20) | copy-start | bytes 12292
  1.9 17.4 %copy-start.47 = (s32[12]{0:T(128)S(1)}, s32[12]{0:T(128)}, u32[]{:S(2)}) copy-start(s32[12]{0:T(128)} %param.16) | copy-start | bytes 148
  67.8 3.6 copy-start.17
  114.4 3.4 copy-start.6
  145.2 30.8 %copy-start.40 = (f32[16]{0:T(128)S(1)}, f32[16]{0:T(128)}, u32[]{:S(2)}) copy-start(f32[16]{0:T(128)} %get-tuple-element.34) | copy-start | bytes 196
  145.2 30.8 %copy-start.41 = (f32[16]{0:T(128)S(1)}, f32[16]{0:T(128)}, u32[]{:S(2)}) copy-start(f32[16]{0:T(128)} %get-tuple-element.38) | copy-start | bytes 196
  175.3 13.3 %copy-start.13 = (bf16[1024,512]{1,0:T(8,128)(2,1)S(1)}, bf16[1024,512]{1,0:T(8,128)(2,1)}, u32[]{:S(2)}) copy-start(bf16[1024,512]{1,0:T(8,128)(2,1)} %param.27) | copy-start | bytes 3145732
  176.8 12.2 %copy-start.19 = (bf16[128,512]{1,0:T(8,128)(2,1)}, bf16[128,512]{1,0:T(8,128)(2,1)S(1)}, u32[]{:S(2)}) copy-start(bf16[128,512]{1,0:T(8,128)(2,1)S(1)} %multiply_convert_fusion.3) | copy-start | bytes 393220
  177.1 34.9 %copy-start.28 = (bf16[128,64]{0,1:T(8,128)(2,1)S(1)}, bf16[128,64]{0,1:T(8,128)(2,1)}, u32[]{:S(2)}) copy-start(bf16[128,64]{0,1:T(8,128)(2,1)} %copy-done.27) | copy-start | bytes 49156
  231.9 2.8 copy-start.29
  237.0 2.8 copy-start.10
  237.0 2.8 copy-start.37
  237.0 2.8 copy-start.45
  243.2 3.5 copy-start.30
  243.2 3.5 copy-start.38
  243.2 3.5 copy-start.46
  263.2 44.2 %copy-start.25 = (bf16[128,64]{1,0:T(8,128)(2,1)S(1)}, bf16[128,64]{1,0:T(8,128)(2,1)}, u32[]{:S(2)}) copy-start(bf16[128,64]{1,0:T(8,128)(2,1)} %copy.57) | copy-start | bytes 49156
  307.5 22.1 %copy-start.12 = (bf16[1024,3,128]{0,2,1:T(8,128)(2,1)S(1)}, bf16[1024,3,128]{0,2,1:T(8,128)(2,1)}, u32[]{:S(2)}) copy-start(bf16[1024,3,128]{0,2,1:T(8,128)(2,1)} %copy-done.11) | copy-start | bytes 2359300
  307.9 34.2 %copy-start.32 = (f32[16]{0:T(128)S(1)}, f32[16]{0:T(128)}, u32[]{:S(2)}) copy-start(f32[16]{0:T(128)} %copy-done.31) | copy-start | bytes 196
  307.9 34.2 %copy-start.33 = (f32[16]{0:T(128)S(1)}, f32[16]{0:T(128)}, u32[]{:S(2)}) copy-start(f32[16]{0:T(128)} %get-tuple-element.54) | copy-start | bytes 196
  328.8 23.2 %copy-start.20 = (bf16[128,512]{1,0:T(8,128)(2,1)S(1)}, bf16[128,512]{1,0:T(8,128)(2,1)}, u32[]{:S(2)}) copy-start(bf16[128,512]{1,0:T(8,128)(2,1)} %copy-done.19) | copy-start | bytes 393220
  328.8 23.2 %copy-start.24 = (bf16[128,1024]{1,0:T(8,128)(2,1)S(1)}, bf16[128,1024]{1,0:T(8,128)(2,1)}, u32[]{:S(2)}) copy-start(bf16[128,1024]{1,0:T(8,128)(2,1)} %param.29) | copy-start | bytes 786436
  (24 other events, 37.7 us)

commit v2 on v1

v2 whole, which is shorter than its diff:
```python
import functools
import jax
import jax.numpy as jnp
from jax import lax
from jax.experimental import pallas as pl
from jax.experimental.pallas import tpu as pltpu
from jax.sharding import PartitionSpec as P

D = 1024
H = 16
DH = 64
V = 96
NV = 8
CHIPS = 16
SLOTS = V // NV
ROWS = 128
PART = ROWS // NV
HID = 512
KEYS = 4096
HALF = KEYS // 2
CHUNK = 512
EPSILON = 1e-05
MASK_FLOOR = -1e30
MESH = pl.DeviceIdType.MESH
bf16, f32 = jnp.bfloat16, jnp.float32
FAR_FIRST = (4, 3, 5, 2, 6, 1, 7)


def nn(a, b):
    return jnp.dot(a, b, preferred_element_type=f32)


def nt(a, b):
    return lax.dot_general(a, b, (((1,), (1,)), ((), ())), preferred_element_type=f32)


def tn(a, b):
    return lax.dot_general(a, b, (((0,), (0,)), ((), ())), preferred_element_type=f32)


def mean(values):
    return jnp.mean(values, -1, keepdims=True)


def layer_norm(inputs):
    values = inputs.astype(f32)
    centred = values - mean(values)
    return centred * lax.rsqrt(mean(centred * centred) + EPSILON)


def norm_back(inputs, upstream):
    values = inputs.astype(f32)
    centred = values - mean(values)
    inv_std = lax.rsqrt(mean(centred * centred) + EPSILON)
    normed = centred * inv_std
    return inv_std * (upstream - mean(upstream) - normed * mean(upstream * normed))


def thirds(wide, lane):
    high = wide.astype(bf16).astype(f32)
    rest = wide - high
    middle = rest.astype(bf16).astype(f32)
    low = rest - middle
    picked = jnp.where(lane < H, high, jnp.where(lane < 2 * H, middle, low))
    return jnp.where(lane < 3 * H, picked, 0.0).astype(bf16)


def iota(shape, dim):
    return lax.broadcasted_iota(jnp.int32, shape, dim)


SCRATCH = dict(
    pixels=((SLOTS, 64, ROWS), bf16),
    embed_w=((SLOTS, 64, D), bf16),
    table=((V, D), bf16),
    agg_key=((32, D), bf16),
    agg_value=((D, D), bf16),
    agg_out=((D, D), bf16),
    pos=((ROWS, D), bf16),
    w_qkv=((D, 384), bf16),
    w_out=((ROWS, D), bf16),
    w_up=((D, HID), bf16),
    w_down=((HID, D), bf16),
    cot=((ROWS, D), bf16),
    table_rows=((16, D), f32),
    embedded=((SLOTS * ROWS, D), bf16),
    values=((SLOTS * ROWS, D), f32),
    dirs_part=((32, 128), bf16),
    dirs_land=((2, CHIPS, 32, 128), bf16),
    dirs=((D, 128), bf16),
    scores=((SLOTS * ROWS, 128), f32),
    shares=((SLOTS * ROWS, 128), bf16),
    pooled=((ROWS, D), bf16),
    level=((ROWS, 128), f32),
    pooled_land=((7, PART, D), bf16),
    level_land=((7, PART, 128), f32),
    tokens=((ROWS, D), bf16),
    normed_in=((ROWS, D), bf16),
    keys=((KEYS, 128), bf16),
    vals=((KEYS, 128), bf16),
    q_two=((256, 128), bf16),
    d_two=((256, 128), bf16),
    probs=((KEYS, 256), f32),
    probs_b=((KEYS, 256), bf16),
    grad_probs=((KEYS, 256), f32),
    context=((ROWS, 128), bf16),
    attn=((ROWS, D), bf16),
    attn_land=((7, PART, D), bf16),
    middle=((ROWS, D), bf16),
    normed_mid=((ROWS, D), bf16),
    upstream=((ROWS, HID), f32),
    activated=((ROWS, HID), bf16),
    grad_pre=((ROWS, HID), bf16),
    gmid=((ROWS, D), bf16),
    gmid_land=((7, PART, D), bf16),
    down=((ROWS, D), bf16),
    down_land=((7, PART, D), bf16),
    layer=((ROWS, D), bf16),
    grad_middle=((ROWS, D), bf16),
    gk=((KEYS, 128), bf16),
    gv=((KEYS, 128), bf16),
    gk_sib=((HALF, 128), bf16),
    gv_sib=((HALF, 128), bf16),
    gk_sum=((CHIPS, 128, 128), bf16),
    gv_sum=((CHIPS, 128, 128), bf16),
    gk_land=((CHIPS - 1, 128, 128), bf16),
    gv_land=((CHIPS - 1, 128, 128), bf16),
    grad_rows=((ROWS, 384), bf16),
    gin=((ROWS, D), bf16),
    gin_land=((7, PART, D), bf16),
    grad_tok=((ROWS, D), bf16),
)
WEIGHT_GRADS = dict(down=(16, D), up=(32, HID), out=(16, 256), qkv=(32, 384))
for _name, (_r, _w) in WEIGHT_GRADS.items():
    SCRATCH["wg_part_" + _name] = ((32 * _r, _w), bf16)
    SCRATCH["wg_sib_" + _name] = ((CHIPS, _r, _w), bf16)
    SCRATCH["wg_sum_" + _name] = ((CHIPS, _r, _w), bf16)
    SCRATCH["wg_land_" + _name] = ((CHIPS - 1, _r, _w), bf16)
LOADED = ("agg_key", "pixels", "embed_w", "table", "agg_value", "agg_out", "pos", "w_qkv",
          "w_out", "w_up", "w_down", "cot")
SEMS = 160


class Names:
    pass


def whole_kernel(*refs):
    mask_ref, ids_ref, query_ref = refs[:3]
    hbm = dict(zip(LOADED, refs[3 : 3 + len(LOADED)]))
    at = 3 + len(LOADED)
    layer_ref, gtok_ref, gqkv_ref, gout_ref, gup_ref, gdown_ref = refs[at : at + 6]
    at += 6
    b = Names()
    for name, ref in zip(SCRATCH, refs[at : at + len(SCRATCH)]):
        setattr(b, name, ref)
    load_sem, ss, rs = refs[at + len(SCRATCH) :]

    v = lax.axis_index("var")
    s = lax.axis_index("space")
    core = lax.rem(s, 2)
    chip = s // 2
    cx, cy = chip // 4, lax.rem(chip, 4)
    sib = s + 1 - 2 * core
    own = pl.ds(pl.multiple_of(v * PART, PART), PART)

    def chip_at(dx, dy):
        return lax.rem(cx + dx, 4) * 4 + lax.rem(cy + dy, 4)

    offsets = [(dx, dy) for dx in range(4) for dy in range(4)]
    around = {o: chip_at(*o) for o in offsets}

    used = [0]
    pending = []

    def fresh(n=1):
        used[0] += n
        assert used[0] <= SEMS
        return used[0] - n

    def wait(sem, ref):
        pltpu.make_async_copy(ref, ref, sem).wait()

    def send(src, dst, k, where):
        pltpu.make_async_remote_copy(
            src_ref=src, dst_ref=dst, send_sem=ss.at[k], recv_sem=rs.at[k],
            device_id=where, device_id_type=MESH,
        ).start()

    def to_core(c):
        return {"space": c}

    def same_core(o):
        return {"space": around[o] * 2 + core}

    loads = {}
    for i, name in enumerate(LOADED):
        loads[name] = pltpu.make_async_copy(hbm[name], getattr(b, name), load_sem.at[i])
        loads[name].start()

    def ready(*names):
        for name in names:
            loads[name].wait()

    barrier = pltpu.get_barrier_semaphore()
    for d in range(1, 8):
        pl.semaphore_signal(barrier, inc=1, device_id={"var": lax.rem(v + d, NV)}, device_id_type=MESH)
    for o in offsets[1:]:
        pl.semaphore_signal(barrier, inc=1, device_id=same_core(o), device_id_type=MESH)
    pl.semaphore_signal(barrier, inc=1, device_id=to_core(sib), device_id_type=MESH)

    def z_scatter(src, land):
        k = fresh()
        for d in FAR_FIRST:
            there = lax.rem(v + d, NV)
            send(src.at[pl.ds(pl.multiple_of(there * PART, PART), PART)], land.at[d - 1], k,
                 {"var": there})
        pending.append((k, land))
        return lambda: wait(rs.at[k], land)

    def z_gather(ref):
        k = fresh()
        for d in FAR_FIRST:
            send(ref.at[own], ref.at[own], k, {"var": lax.rem(v + d, NV)})
        pending.append((k, ref.at[pl.ds(0, 7 * PART)]))
        return lambda: wait(rs.at[k], ref.at[pl.ds(0, 7 * PART)])

    def landed(src, land):
        total = src[own].astype(f32)
        for d in range(7):
            total = total + land[d].astype(f32)
        return total

    class Reduce:
        def __init__(self, name):
            self.part = getattr(b, "wg_part_" + name)
            self.sib = getattr(b, "wg_sib_" + name)
            self.sum = getattr(b, "wg_sum_" + name)
            self.land = getattr(b, "wg_land_" + name)
            self.r = WEIGHT_GRADS[name][0]
            self.k = fresh(2)

        def block(self, which, side):
            return pl.ds(pl.multiple_of((2 * which + side) * self.r, self.r), self.r)

        def start(self):
            for i in range(CHIPS):
                send(self.part.at[self.block(i, 1 - core)], self.sib.at[i], self.k, to_core(sib))
            pending.append((self.k, self.sib))

        def spread(self):
            wait(rs.at[self.k], self.sib)

            def add(i, carry):
                self.sum[i] = (self.part[self.block(i, core)].astype(f32)
                               + self.sib[i].astype(f32)).astype(bf16)
                return carry

            lax.fori_loop(0, CHIPS, add, 0)
            for j, o in enumerate(offsets[1:]):
                send(self.sum.at[around[o]], self.land.at[j], self.k + 1, same_core(o))
            pending.append((self.k + 1, self.land))

        def finish(self):
            wait(rs.at[self.k + 1], self.land)
            total = self.part[self.block(chip, core)].astype(f32) + self.sib[chip].astype(f32)
            for j in range(CHIPS - 1):
                total = total + self.land[j].astype(f32)
            return total

    ready("agg_key")
    row, lane = iota((128, D), 0), iota((128, D), 1)
    spots = (lane // DH == lax.rem(row, H)) & (row < 3 * H)
    spread_one = jnp.where(spots, 1.0, 0.0).astype(bf16)
    rest = jnp.where(spots, query_ref[...], 0.0)
    dirs = jnp.zeros((32, 128), f32)
    for _ in range(3):
        piece = rest.astype(bf16)
        dirs = dirs + nt(b.agg_key[...], piece)
        rest = rest - piece.astype(f32)
    b.dirs_part[...] = dirs.astype(bf16)
    b.dirs_land[0, 0] = dirs.astype(bf16)

    pl.semaphore_wait(barrier, 7 + CHIPS - 1 + 1)
    dirs_k = fresh(2)
    for j, o in enumerate(offsets[1:]):
        send(b.dirs_part, b.dirs_land.at[0, j + 1], dirs_k, same_core(o))
    pending.append((dirs_k, b.dirs_land.at[0, pl.ds(1, CHIPS - 1)]))

    ready("table")
    row, lane = iota((16, V), 0), iota((16, V), 1)
    picks = jnp.zeros((16, V), f32)
    for i in range(SLOTS):
        picks = picks + jnp.where((row == i) & (lane == ids_ref[i]), 1.0, 0.0)
    b.table_rows[...] = nn(picks.astype(bf16), b.table[...])
    ready("pixels", "embed_w")

    def embed(i, carry):
        raw = tn(b.pixels[i], b.embed_w[i])
        b.embedded[pl.ds(pl.multiple_of(i * ROWS, ROWS), ROWS)] = (
            raw + b.table_rows[pl.ds(i, 1)]).astype(bf16)
        return carry

    lax.fori_loop(0, SLOTS, embed, 0)
    wait(rs.at[dirs_k], b.dirs_land.at[0, pl.ds(1, CHIPS - 1)])
    send(b.dirs_land.at[0], b.dirs_land.at[1], dirs_k + 1, to_core(sib))
    pending.append((dirs_k + 1, b.dirs_land.at[1]))
    ready("agg_value")

    def value_columns(i, carry):
        columns = pl.ds(pl.multiple_of(i * 256, 256), 256)
        for m in range(2):
            these = pl.ds(m * 768, 768)
            b.values[these, columns] = nn(b.embedded[these], b.agg_value[:, columns])
        return carry

    lax.fori_loop(0, 4, value_columns, 0)
    wait(rs.at[dirs_k + 1], b.dirs_land.at[1])
    for j, o in enumerate(offsets):
        source = lax.rem(cx - o[0] + 4, 4) * 4 + lax.rem(cy - o[1] + 4, 4)
        for side in range(2):
            owner = 2 * source + (core if side == 0 else 1 - core)
            b.dirs[pl.ds(pl.multiple_of(owner * 32, 32), 32)] = b.dirs_land[side, j]

    b.scores[...] = nn(b.embedded[...], b.dirs[...]) * DH ** (-0.5)
    lane = iota((ROWS, 128), 1)
    top = jnp.full((ROWS, 128), MASK_FLOOR, f32)
    for i in range(SLOTS):
        rows = pl.ds(i * ROWS, ROWS)
        top = jnp.maximum(top, jnp.where(mask_ref[i] > 0, b.scores[rows], MASK_FLOOR))
    total = jnp.zeros((ROWS, 128), f32)
    for i in range(SLOTS):
        rows = pl.ds(i * ROWS, ROWS)
        weight = jnp.where(mask_ref[i] > 0, jnp.exp(
            jnp.where(mask_ref[i] > 0, b.scores[rows], MASK_FLOOR) - top), 0.0)
        b.scores[rows] = weight
        total = total + weight
    scale = 1.0 / total
    b.level[...] = top + jnp.log(total)
    for i in range(SLOTS):
        rows = pl.ds(i * ROWS, ROWS)
        b.shares[rows] = thirds(b.scores[rows] * scale, lane)
    for c in range(4):
        columns = slice(c * 256, (c + 1) * 256)
        acc = jnp.zeros((ROWS, 256), f32)
        for i in range(SLOTS):
            rows = pl.ds(i * ROWS, ROWS)
            acc = acc + nn(b.shares[rows], spread_one[:, columns]) * b.values[rows, columns]
        b.pooled[:, columns] = acc.astype(bf16)
    level_in = z_scatter(b.level, b.level_land)
    pooled_in = z_scatter(b.pooled, b.pooled_land)

    ready("w_down", "cot")
    b.upstream[...] = nt(b.cot[...], b.w_down[...])
    ready("agg_out", "pos")
    level_in()
    levels = [b.level[own]] + [b.level_land[d] for d in range(7)]
    top = functools.reduce(jnp.maximum, levels)
    lifts = [jnp.exp(x - top) for x in levels]
    scale = 1.0 / sum(lifts[1:], lifts[0])
    lane = iota((PART, 128), 1)
    lifts = [nn(thirds(x * scale, lane), spread_one) for x in lifts]
    pooled_in()
    mixed = lifts[0] * b.pooled[own].astype(f32)
    for d in range(7):
        mixed = mixed + lifts[d + 1] * b.pooled_land[d].astype(f32)
    b.tokens[own] = (nn(mixed.astype(bf16), b.agg_out[...]) + b.pos[own].astype(f32)).astype(bf16)
    tokens_in = z_gather(b.tokens)
    ready("w_qkv", "w_out", "w_up")
    tokens_in()

    b.normed_in[...] = layer_norm(b.tokens[...]).astype(bf16)
    qkv = nn(b.normed_in[...], b.w_qkv[...]).astype(bf16)
    b.keys[pl.ds(0, ROWS)] = qkv[:, 128:256]
    b.vals[pl.ds(0, ROWS)] = qkv[:, 256:]
    slot = lambda dx, dy, side=0: pl.ds(((side * 4 + dx) * 4 + dy) * ROWS, ROWS)
    first = fresh(12)
    for i in range(1, 4):
        send(b.keys.at[slot(0, 0)], b.keys.at[slot(i, 0)], first + i - 1, same_core((i, 0)))
        send(b.vals.at[slot(0, 0)], b.vals.at[slot(0, i)], first + 2 + i, same_core((0, i)))
    for i in range(1, 4):
        send(b.keys.at[slot(0, 0)], b.keys.at[slot(0, i)], first + 5 + i, same_core((0, i)))
        send(b.vals.at[slot(0, 0)], b.vals.at[slot(i, 0)], first + 8 + i, same_core((i, 0)))
    block = b.keys.at[slot(0, 0)]
    for i in range(12):
        pending.append((first + i, block))
    mine = fresh()
    send(b.keys.at[slot(0, 0)], b.keys.at[slot(0, 0, 1)], mine, to_core(sib))
    send(b.vals.at[slot(0, 0)], b.vals.at[slot(0, 0, 1)], mine, to_core(sib))
    twice = b.keys.at[pl.ds(0, 2 * ROWS)]
    pending.append((mine, twice))
    query = qkv[:, :128] * DH ** (-0.5)
    lane = iota((ROWS, 128), 1)
    zero = jnp.zeros((ROWS, 128), bf16)
    b.q_two[pl.ds(0, ROWS)] = jnp.where(lane < DH, query, zero)
    b.q_two[pl.ds(ROWS, ROWS)] = jnp.where(lane < DH, zero, query)
    second = {}
    for i in range(1, 4):
        wait(rs.at[first + i - 1], block)
        for j in range(1, 4):
            second["k", i, j] = k = fresh()
            send(b.keys.at[slot(i, 0)], b.keys.at[slot(i, j)], k, same_core((0, j)))
        wait(rs.at[first + 2 + i], block)
        for j in range(1, 4):
            second["v", j, i] = k = fresh()
            send(b.vals.at[slot(0, i)], b.vals.at[slot(j, i)], k, same_core((j, 0)))
    for i in range(1, 4):
        wait(rs.at[first + 5 + i], block)
        wait(rs.at[first + 8 + i], block)
    fours = fresh()
    send(b.keys.at[pl.ds(ROWS, 3 * ROWS)], b.keys.at[pl.ds(HALF + ROWS, 3 * ROWS)], fours, to_core(sib))
    send(b.vals.at[pl.ds(ROWS, 3 * ROWS)], b.vals.at[pl.ds(HALF + ROWS, 3 * ROWS)], fours, to_core(sib))
    pending.append((fours, b.keys.at[pl.ds(0, 6 * ROWS)]))
    sides = [fours]
    for i in range(1, 4):
        for j in range(1, 4):
            wait(rs.at[second["k", i, j]], block)
            wait(rs.at[second["v", i, j]], block)
            pending.append((second["k", i, j], block))
            pending.append((second["v", i, j], block))
        k = fresh()
        rows = pl.ds(i * 4 * ROWS, 4 * ROWS)
        over = pl.ds(HALF + i * 4 * ROWS, 4 * ROWS)
        send(b.keys.at[rows], b.keys.at[over], k, to_core(sib))
        send(b.vals.at[rows], b.vals.at[over], k, to_core(sib))
        pending.append((k, b.keys.at[pl.ds(0, 8 * ROWS)]))
        sides.append(k)
    wait(rs.at[mine], twice)
    wait(rs.at[sides[0]], b.keys.at[pl.ds(0, 6 * ROWS)])
    for k in sides[1:]:
        wait(rs.at[k], b.keys.at[pl.ds(0, 8 * ROWS)])

    def chunk(i):
        return pl.ds(pl.multiple_of(i * CHUNK, CHUNK), CHUNK)

    def eights(x):
        return x.reshape(CHUNK // 8, 8, 256)

    def score_step(i, top):
        part = nt(b.keys[chunk(i)], b.q_two[...])
        b.probs[chunk(i)] = part
        return jnp.maximum(top, jnp.max(eights(part), 0))

    top = lax.fori_loop(0, KEYS // CHUNK, score_step, jnp.full((8, 256), -jnp.inf, f32))
    top = jnp.max(top, 0, keepdims=True)

    def exp_step(i, total):
        part = jnp.exp(b.probs[chunk(i)] - top)
        b.probs[chunk(i)] = part
        return total + jnp.sum(eights(part), 0)

    total = lax.fori_loop(0, KEYS // CHUNK, exp_step, jnp.zeros((8, 256), f32))
    scale = 1.0 / jnp.sum(total, 0, keepdims=True)

    def context_step(i, acc):
        part = b.probs[chunk(i)] * scale
        b.probs[chunk(i)] = part
        b.probs_b[chunk(i)] = part.astype(bf16)
        return acc + tn(b.vals[chunk(i)], part.astype(bf16))

    acc = lax.fori_loop(0, KEYS // CHUNK, context_step, jnp.zeros((128, 256), f32))
    tall = iota((128, 128), 0)
    b.context[...] = jnp.where(tall < DH, acc[:, :128], acc[:, 128:]).T.astype(bf16)

    b.attn[...] = nn(b.context[...], b.w_out[...]).astype(bf16)
    attn_in = z_scatter(b.attn, b.attn_land)
    attn_in()
    b.middle[own] = (b.tokens[own].astype(f32) + landed(b.attn, b.attn_land)).astype(bf16)
    middle_in = z_gather(b.middle)
    middle_in()

    b.normed_mid[...] = layer_norm(b.middle[...]).astype(bf16)
    pre = nn(b.normed_mid[...], b.w_up[...])
    half = 0.5 * (1.0 + lax.erf(pre * 0.5 ** 0.5))
    b.activated[...] = (pre * half).astype(bf16)
    slope = half + pre * (jnp.exp(-0.5 * pre * pre) * 0.3989422804014327)
    b.grad_pre[...] = (b.upstream[...] * slope).astype(bf16)
    b.gmid[...] = nt(b.grad_pre[...], b.w_up[...]).astype(bf16)
    gmid_in = z_scatter(b.gmid, b.gmid_land)
    b.down[...] = nn(b.activated[...], b.w_down[...]).astype(bf16)
    down_in = z_scatter(b.down, b.down_land)
    wg = {name: Reduce(name) for name in WEIGHT_GRADS}
    wg["down"].part[...] = tn(b.activated[...], b.cot[...]).astype(bf16)
    wg["down"].start()
    gmid_in()
    b.grad_middle[own] = (b.cot[own].astype(f32) + norm_back(
        b.middle[own], landed(b.gmid, b.gmid_land))).astype(bf16)
    grad_middle_in = z_gather(b.grad_middle)
    wg["up"].part[...] = tn(b.normed_mid[...], b.grad_pre[...]).astype(bf16)
    wg["up"].start()
    wg["down"].spread()
    grad_middle_in()

    grad_context = nt(b.grad_middle[...], b.w_out[...]).astype(bf16)
    lane = iota((ROWS, 128), 1)
    b.d_two[pl.ds(0, ROWS)] = jnp.where(lane < DH, grad_context, zero)
    b.d_two[pl.ds(ROWS, ROWS)] = jnp.where(lane < DH, zero, grad_context)

    def delta_step(i, total):
        part = nt(b.vals[chunk(i)], b.d_two[...])
        b.grad_probs[chunk(i)] = part
        return total + jnp.sum(eights(part * b.probs[chunk(i)]), 0)

    delta = lax.fori_loop(0, KEYS // CHUNK, delta_step, jnp.zeros((8, 256), f32))
    delta = jnp.sum(delta, 0, keepdims=True)

    def back_step(i, acc):
        grad = (b.probs[chunk(i)] * (b.grad_probs[chunk(i)] - delta)).astype(bf16)
        b.gk[chunk(i)] = nn(grad, b.q_two[...]).astype(bf16)
        b.gv[chunk(i)] = nn(b.probs_b[chunk(i)], b.d_two[...]).astype(bf16)
        return acc + tn(b.keys[chunk(i)], grad)

    halves = KEYS // CHUNK // 2
    acc = lax.fori_loop(halves, 2 * halves, back_step, jnp.zeros((128, 256), f32))
    kv_k = fresh(2)
    send(b.gk.at[pl.ds(HALF, HALF)], b.gk_sib, kv_k, to_core(sib))
    send(b.gv.at[pl.ds(HALF, HALF)], b.gv_sib, kv_k, to_core(sib))
    pending.append((kv_k, b.gk))
    acc = lax.fori_loop(0, halves, back_step, acc)
    wait(rs.at[kv_k], b.gk)

    def pair_step(i, carry):
        rows = pl.ds(pl.multiple_of(i * ROWS, ROWS), ROWS)
        b.gk_sum[i] = (b.gk[rows].astype(f32) + b.gk_sib[rows].astype(f32)).astype(bf16)
        b.gv_sum[i] = (b.gv[rows].astype(f32) + b.gv_sib[rows].astype(f32)).astype(bf16)
        return carry

    lax.fori_loop(0, CHIPS, pair_step, 0)
    for j, o in enumerate(offsets):
        if j:
            back = same_core(((4 - o[0]) % 4, (4 - o[1]) % 4))
            send(b.gk_sum.at[j], b.gk_land.at[j - 1], kv_k + 1, back)
            send(b.gv_sum.at[j], b.gv_land.at[j - 1], kv_k + 1, back)
    both = b.gk.at[pl.ds(0, 2 * (CHIPS - 1) * ROWS)]
    pending.append((kv_k + 1, both))

    grad_query = jnp.where(tall < DH, acc[:, :128], acc[:, 128:]).T * DH ** (-0.5)
    b.grad_rows[:, :128] = grad_query.astype(bf16)
    down_in()
    b.layer[own] = (b.middle[own].astype(f32) + landed(b.down, b.down_land)).astype(bf16)
    layer_in = z_gather(b.layer)
    wg["up"].spread()
    row, lane = iota((128, 512), 0), iota((128, 512), 1)
    total = jnp.zeros((512, 256), f32)
    for q in range(4):
        pick = (lane // 16 == row // 4) & (lax.rem(lane, 16) == q * 4 + lax.rem(row, 4))
        picked = nn(b.context[...], jnp.where(pick, 1.0, 0.0).astype(bf16)).astype(bf16)
        total = total + tn(picked, b.grad_middle[:, q * 256 : (q + 1) * 256])
    wg["out"].part[...] = total.astype(bf16)
    wg["out"].start()
    layer_in()
    layer_ref[...] = b.layer[...]
    gdown_ref[...] = wg["down"].finish()
    wg["out"].spread()

    wait(rs.at[kv_k + 1], both)
    for c, part, other, land in ((1, b.gk, b.gk_sib, b.gk_land), (2, b.gv, b.gv_sib, b.gv_land)):
        rows = pl.ds(0, ROWS)
        total = part[rows].astype(f32) + other[rows].astype(f32)
        for j in range(CHIPS - 1):
            total = total + land[j].astype(f32)
        b.grad_rows[:, c * 128 : (c + 1) * 128] = total.astype(bf16)

    b.gin[...] = nt(b.grad_rows[...], b.w_qkv[...]).astype(bf16)
    gin_in = z_scatter(b.gin, b.gin_land)
    wg["qkv"].part[...] = tn(b.normed_in[...], b.grad_rows[...]).astype(bf16)
    wg["qkv"].start()
    wg["qkv"].spread()
    gin_in()
    b.grad_tok[own] = (b.grad_middle[own].astype(f32) + norm_back(
        b.tokens[own], landed(b.gin, b.gin_land))).astype(bf16)
    grad_tok_in = z_gather(b.grad_tok)
    gup_ref[...] = wg["up"].finish()
    total = wg["out"].finish()
    for q in range(4):
        gout_ref[:, q * 256 : (q + 1) * 256] = total[q * 4 : (q + 1) * 4]
    total = wg["qkv"].finish()
    for c in range(3):
        gqkv_ref[:, c, :] = total[:, c * 128 : (c + 1) * 128]
    grad_tok_in()
    gtok_ref[...] = b.grad_tok[...]
    for k, ref in pending:
        wait(ss.at[k], ref)


def shards(pixels, valid_mask, var_ids, embed_weight, var_table, agg_query, agg_key,
           agg_value, agg_out, pos_embed, w_qkv, w_out, w_up, w_down, cotangent):
    in_vmem = pl.BlockSpec(memory_space=pltpu.VMEM)
    in_smem = pl.BlockSpec(memory_space=pltpu.SMEM)
    anywhere = pl.BlockSpec(memory_space=pl.ANY)
    big = (agg_key, pixels, embed_weight, var_table, agg_value, agg_out, pos_embed,
           w_qkv.reshape(D, 384), w_out, w_up, w_down, cotangent)
    shape = jax.ShapeDtypeStruct
    return tuple(pl.pallas_call(
        whole_kernel,
        out_shape=[shape((ROWS, D), bf16), shape((ROWS, D), bf16), shape((32, 3, 128), f32),
                   shape((4, D), f32), shape((32, HID), f32), shape((16, D), f32)],
        in_specs=[in_smem, in_smem, in_vmem] + [anywhere] * len(big),
        out_specs=[in_vmem] * 6,
        scratch_shapes=[pltpu.VMEM(*spec) for spec in SCRATCH.values()]
        + [pltpu.SemaphoreType.DMA((len(LOADED),)), pltpu.SemaphoreType.DMA((SEMS,)),
           pltpu.SemaphoreType.DMA((SEMS,))],
        compiler_params=pltpu.CompilerParams(
            collective_id=0, has_side_effects=True, vmem_limit_bytes=60 * 2**20),
        name="whole",
    )(valid_mask, var_ids, agg_query.reshape(1, D), *big))


def solution(mesh):
    in_specs = (
        P("var", None, "space"), P("var"), P("var"), P("var", None, None), P(), P(),
        P("space", None), P(), P(), P("space", None), P(None, None, "var"), P("var", None),
        P(None, "var"), P("var", None), P("space", None),
    )
    out_specs = (
        P("space", None), P("space", None), P("space", None, "var"),
        P(("var", "space"), None), P("space", "var"), P(("var", "space"), None),
    )
    return jax.shard_map(shards, mesh=mesh, in_specs=in_specs, out_specs=out_specs, check_vma=False)
```

time: 392 us -> 149 us (0.38)
  the two profiles are of different devices: /device:TPU:1 before, /device:TPU:3 now
where the time goes in v2:
time: 149 us; the launch traced here: 148 us
  Pallas kernels  136 us (91%)
  local copies, waits for them, and re-layouts  11.6 us (8%)
    pallas_call x1, Pallas kernels, shards(): pl.pallas_call(whole_kernel, out_shape=[shape((ROWS, D), bf16), shape((RO...  136 us
    unnamed x6, local copies, waits for them, and re-layouts  9.01 us

profile of v2, /device:TPU:3, one launch (start us, length us, event | category | flops | bytes accessed | tf_op | source)
XLA Modules:
  0.0 148.3 jit_solution(4985661007021753781)
XLA Ops:
  0.6 1.4 copy.23
  2.0 1.2 copy.24.refs_10_
  3.2 136.0 %whole.1 = (bf16[128,1024]{1,0:T(8,128)(2,1)}, bf16[128,1024]{1,0:T(8,128)(2,1)}, f32[32,3,128]{2,1,0:T(4,128)}, f32[4,1024]{1,0:T(4,128)}, f32[32,512]{1,0:T(8,128)}, /*index=5*/f32[16,1024]{1,0:T(8,128)}) custom-call(s32[12]{0:T(128)} %refs_0_.1, s32[12]{0:T(128)} %refs_1_.1, f32[1,1024]{1,0:T(1,128)} %bitcast.3, bf16[32,1024]{1,0:T(8,128)(2,1)} %refs_3_.1, ...), custom_call_target="tpu_custom_call" | custom-call | tf_op jit(solution)/shard_map/whole/pallas_call | solution.py:594
  139.2 1.5 copy.25
  140.7 1.7 %copy.31 = bf16[128,1024]{1,0:T(8,128)(2,1)} copy(bf16[128,1024]{1,0:T(8,128)(2,1)} %get-tuple-element.24) | data formatting | bytes 524288
  142.3 1.7 %copy.32 = bf16[128,1024]{1,0:T(8,128)(2,1)} copy(bf16[128,1024]{1,0:T(8,128)(2,1)} %get-tuple-element.25) | data formatting | bytes 524288
  144.0 1.3 copy.33
  145.3 1.5 copy.34
  146.8 1.5 copy.35

commit v3 on v2

--- a/solution.py
+++ b/solution.py
@@ -16,9 +16,11 @@
 ROWS = 128
 PART = ROWS // NV
 HID = 512
-KEYS = 4096
-HALF = KEYS // 2
-CHUNK = 512
+RING = 4
+TEAM = 8
+KEYS = RING * ROWS
+ASKED = 2 * TEAM * ROWS
+CHUNK = 128
 EPSILON = 1e-05
 MASK_FLOOR = -1e30
 MESH = pl.DeviceIdType.MESH
@@ -77,7 +79,7 @@
     agg_value=((D, D), bf16),
     agg_out=((D, D), bf16),
     pos=((ROWS, D), bf16),
-    w_qkv=((D, 384), bf16),
+    w_qkv=((3, D, 128), bf16),
     w_out=((ROWS, D), bf16),
     w_up=((D, HID), bf16),
     w_down=((HID, D), bf16),
@@ -98,11 +100,18 @@
     normed_in=((ROWS, D), bf16),
     keys=((KEYS, 128), bf16),
     vals=((KEYS, 128), bf16),
-    q_two=((256, 128), bf16),
-    d_two=((256, 128), bf16),
-    probs=((KEYS, 256), f32),
-    probs_b=((KEYS, 256), bf16),
-    grad_probs=((KEYS, 256), f32),
+    asked=((TEAM, ROWS, 128), bf16),
+    q_two=((ASKED, 128), bf16),
+    graded=((TEAM, 128, ROWS), bf16),
+    d_two=((ASKED, 128), bf16),
+    probs=((KEYS, ASKED), f32),
+    probs_b=((KEYS, ASKED), bf16),
+    grad_probs=((KEYS, ASKED), f32),
+    spans=((TEAM, 2 * TEAM, 128), f32),
+    deltas=((TEAM, 2 * TEAM, 128), f32),
+    flat=((2, 2 * TEAM, 128), f32),
+    shared=((TEAM, 128, ROWS), bf16),
+    shared_land=((TEAM, 128, ROWS), bf16),
     context=((ROWS, 128), bf16),
     attn=((ROWS, D), bf16),
     attn_land=((7, PART, D), bf16),
@@ -117,14 +126,12 @@
     down_land=((7, PART, D), bf16),
     layer=((ROWS, D), bf16),
     grad_middle=((ROWS, D), bf16),
-    gk=((KEYS, 128), bf16),
-    gv=((KEYS, 128), bf16),
-    gk_sib=((HALF, 128), bf16),
-    gv_sib=((HALF, 128), bf16),
-    gk_sum=((CHIPS, 128, 128), bf16),
-    gv_sum=((CHIPS, 128, 128), bf16),
-    gk_land=((CHIPS - 1, 128, 128), bf16),
-    gv_land=((CHIPS - 1, 128, 128), bf16),
+    gq=((TEAM, 128, ROWS), bf16),
+    gq_land=((TEAM - 1, 128, ROWS), bf16),
+    gk=((RING, ROWS, 128), bf16),
+    gv=((RING, ROWS, 128), bf16),
+    gk_land=((RING - 1, ROWS, 128), bf16),
+    gv_land=((RING - 1, ROWS, 128), bf16),
     grad_rows=((ROWS, 384), bf16),
     gin=((ROWS, D), bf16),
     gin_land=((7, PART, D), bf16),
@@ -208,6 +215,8 @@
     for o in offsets[1:]:
         pl.semaphore_signal(barrier, inc=1, device_id=same_core(o), device_id_type=MESH)
     pl.semaphore_signal(barrier, inc=1, device_id=to_core(sib), device_id_type=MESH)
+    for d in range(1, RING):
+        pl.semaphore_signal(barrier, inc=1, device_id=to_core(around[0, d] * 2 + 1 - core), device_id_type=MESH)
 
     def z_scatter(src, land):
         k = fresh()
@@ -230,6 +239,46 @@
         for d in range(7):
             total = total + land[d].astype(f32)
         return total
+
+    place = cy * 2 + core
+    mates = []
+    for d in range(1, RING):
+        mates.append((around[0, d] * 2 + core, lax.rem(cy + d, 4) * 2 + core))
+        mates.append((around[0, d] * 2 + 1 - core, lax.rem(cy + d, 4) * 2 + 1 - core))
+    mates.append((sib, cy * 2 + 1 - core))
+    ring = [(same_core((d, 0)), lax.rem(cx + d, 4)) for d in range(1, RING)]
+
+    def team_gather(ref):
+        k = fresh()
+        for to, _ in mates:
+            send(ref.at[place], ref.at[place], k, to_core(to))
+        seven = ref.at[pl.ds(0, TEAM - 1)]
+        pending.append((k, seven))
+        return lambda: wait(rs.at[k], seven)
+
+    def team_scatter(src, land):
+        k = fresh()
+        for j, (to, t) in enumerate(mates):
+            send(src.at[t], land.at[j], k, to_core(to))
+        seven = land.at[pl.ds(0, TEAM - 1)]
+        pending.append((k, seven))
+        return lambda: wait(rs.at[k], seven)
+
+    def ring_gather(ref):
+        k = fresh()
+        rows = pl.ds(pl.multiple_of(cx * ROWS, ROWS), ROWS)
+        for to, _ in ring:
+            send(ref.at[rows], ref.at[rows], k, to)
+        three = ref.at[pl.ds(0, 3 * ROWS)]
+        pending.append((k, three))
+        return lambda: wait(rs.at[k], three)
+
+    def ring_scatter(src, land):
+        k = fresh()
+        for j, (to, t) in enumerate(ring):
+            send(src.at[t], land.at[j], k, to)
+        pending.append((k, land))
+        return lambda: wait(rs.at[k], land)
 
     class Reduce:
         def __init__(self, name):
@@ -281,7 +330,7 @@
     b.dirs_part[...] = dirs.astype(bf16)
     b.dirs_land[0, 0] = dirs.astype(bf16)
 
-    pl.semaphore_wait(barrier, 7 + CHIPS - 1 + 1)
+    pl.semaphore_wait(barrier, 7 + CHIPS - 1 + 1 + RING - 1)
     dirs_k = fresh(2)
     for j, o in enumerate(offsets[1:]):
         send(b.dirs_part, b.dirs_land.at[0, j + 1], dirs_k, same_core(o))
@@ -370,100 +419,94 @@
     tokens_in()
 
     b.normed_in[...] = layer_norm(b.tokens[...]).astype(bf16)
-    qkv = nn(b.normed_in[...], b.w_qkv[...]).astype(bf16)
-    b.keys[pl.ds(0, ROWS)] = qkv[:, 128:256]
-    b.vals[pl.ds(0, ROWS)] = qkv[:, 256:]
-    slot = lambda dx, dy, side=0: pl.ds(((side * 4 + dx) * 4 + dy) * ROWS, ROWS)
-    first = fresh(12)
-    for i in range(1, 4):
-        send(b.keys.at[slot(0, 0)], b.keys.at[slot(i, 0)], first + i - 1, same_core((i, 0)))
-        send(b.vals.at[slot(0, 0)], b.vals.at[slot(0, i)], first + 2 + i, same_core((0, i)))
-    for i in range(1, 4):
-        send(b.keys.at[slot(0, 0)], b.keys.at[slot(0, i)], first + 5 + i, same_core((0, i)))
-        send(b.vals.at[slot(0, 0)], b.vals.at[slot(i, 0)], first + 8 + i, same_core((i, 0)))
-    block = b.keys.at[slot(0, 0)]
-    for i in range(12):
-        pending.append((first + i, block))
-    mine = fresh()
-    send(b.keys.at[slot(0, 0)], b.keys.at[slot(0, 0, 1)], mine, to_core(sib))
-    send(b.vals.at[slot(0, 0)], b.vals.at[slot(0, 0, 1)], mine, to_core(sib))
-    twice = b.keys.at[pl.ds(0, 2 * ROWS)]
-    pending.append((mine, twice))
-    query = qkv[:, :128] * DH ** (-0.5)
+    mine = pl.ds(pl.multiple_of(cx * ROWS, ROWS), ROWS)
+    b.asked[place] = nn(b.normed_in[...], b.w_qkv[0]).astype(bf16) * DH ** (-0.5)
+    asked_in = team_gather(b.asked)
+    b.keys[mine] = nn(b.normed_in[...], b.w_qkv[1]).astype(bf16)
+    keys_in = ring_gather(b.keys)
+    b.vals[mine] = nn(b.normed_in[...], b.w_qkv[2]).astype(bf16)
+    vals_in = ring_gather(b.vals)
+
+    def chunk(i):
+        return pl.ds(pl.multiple_of(i * CHUNK, CHUNK), CHUNK)
+
+    def eights(x):
+        return x.reshape(CHUNK // 8, 8, ASKED)
+
+    def stretch(ref, t):
+        return jnp.concatenate([ref[t, pl.ds(r, 1), :] for r in range(2 * TEAM)], 1)
+
     lane = iota((ROWS, 128), 1)
     zero = jnp.zeros((ROWS, 128), bf16)
-    b.q_two[pl.ds(0, ROWS)] = jnp.where(lane < DH, query, zero)
-    b.q_two[pl.ds(ROWS, ROWS)] = jnp.where(lane < DH, zero, query)
-    second = {}
-    for i in range(1, 4):
-        wait(rs.at[first + i - 1], block)
-        for j in range(1, 4):
-            second["k", i, j] = k = fresh()
-            send(b.keys.at[slot(i, 0)], b.keys.at[slot(i, j)], k, same_core((0, j)))
-        wait(rs.at[first + 2 + i], block)
-        for j in range(1, 4):
-            second["v", j, i] = k = fresh()
-            send(b.vals.at[slot(0, i)], b.vals.at[slot(j, i)], k, same_core((j, 0)))
-    for i in range(1, 4):
-        wait(rs.at[first + 5 + i], block)
-        wait(rs.at[first + 8 + i], block)
-    fours = fresh()
-    send(b.keys.at[pl.ds(ROWS, 3 * ROWS)], b.keys.at[pl.ds(HALF + ROWS, 3 * ROWS)], fours, to_core(sib))
-    send(b.vals.at[pl.ds(ROWS, 3 * ROWS)], b.vals.at[pl.ds(HALF + ROWS, 3 * ROWS)], fours, to_core(sib))
-    pending.append((fours, b.keys.at[pl.ds(0, 6 * ROWS)]))
-    sides = [fours]
-    for i in range(1, 4):
-        for j in range(1, 4):
-            wait(rs.at[second["k", i, j]], block)
-            wait(rs.at[second["v", i, j]], block)
-            pending.append((second["k", i, j], block))
-            pending.append((second["v", i, j], block))
-        k = fresh()
-        rows = pl.ds(i * 4 * ROWS, 4 * ROWS)
-        over = pl.ds(HALF + i * 4 * ROWS, 4 * ROWS)
-        send(b.keys.at[rows], b.keys.at[over], k, to_core(sib))
-        send(b.vals.at[rows], b.vals.at[over], k, to_core(sib))
-        pending.append((k, b.keys.at[pl.ds(0, 8 * ROWS)]))
-        sides.append(k)
-    wait(rs.at[mine], twice)
-    wait(rs.at[sides[0]], b.keys.at[pl.ds(0, 6 * ROWS)])
-    for k in sides[1:]:
-        wait(rs.at[k], b.keys.at[pl.ds(0, 8 * ROWS)])
-
-    def chunk(i):
-        return pl.ds(pl.multiple_of(i * CHUNK, CHUNK), CHUNK)
-
-    def eights(x):
-        return x.reshape(CHUNK // 8, 8, 256)
+
+    def two(ref, block):
+        for t in range(TEAM):
+            ref[pl.ds(t * ROWS, ROWS)] = jnp.where(lane < DH, block(t), zero)
+            ref[pl.ds((TEAM + t) * ROWS, ROWS)] = jnp.where(lane < DH, zero, block(t))
+
+    asked_in()
+    two(b.q_two, lambda t: b.asked[t])
+    keys_in()
+    steps = KEYS // CHUNK
 
     def score_step(i, top):
         part = nt(b.keys[chunk(i)], b.q_two[...])
         b.probs[chunk(i)] = part
         return jnp.maximum(top, jnp.max(eights(part), 0))
 
-    top = lax.fori_loop(0, KEYS // CHUNK, score_step, jnp.full((8, 256), -jnp.inf, f32))
+    top = lax.fori_loop(0, steps, score_step, jnp.full((8, ASKED), -jnp.inf, f32))
     top = jnp.max(top, 0, keepdims=True)
 
     def exp_step(i, total):
         part = jnp.exp(b.probs[chunk(i)] - top)
         b.probs[chunk(i)] = part
+        b.probs_b[chunk(i)] = part.astype(bf16)
         return total + jnp.sum(eights(part), 0)
 
-    total = lax.fori_loop(0, KEYS // CHUNK, exp_step, jnp.zeros((8, 256), f32))
-    scale = 1.0 / jnp.sum(total, 0, keepdims=True)
-
-    def context_step(i, acc):
-        part = b.probs[chunk(i)] * scale
+    total = lax.fori_loop(0, steps, exp_step, jnp.zeros((8, ASKED), f32))
+    total = jnp.sum(total, 0, keepdims=True)
+    span = top + jnp.log(total)
+    for r in range(2 * TEAM):
+        b.spans[place, pl.ds(r, 1), :] = span[:, r * 128 : (r + 1) * 128]
+    spans_in = team_gather(b.spans)
+    vals_in()
+    scale = 1.0 / total
+    for h in range(2):
+        side = slice(h * TEAM * ROWS, (h + 1) * TEAM * ROWS)
+        part = tn(b.vals[...], b.probs_b[:, side]) * scale[:, side]
+        for t in range(TEAM):
+            b.shared[t, h * DH : (h + 1) * DH, :] = (
+                part[h * DH : (h + 1) * DH, t * ROWS : (t + 1) * ROWS].astype(bf16))
+    shared_in = team_scatter(b.shared, b.shared_land)
+    spans_in()
+    all_spans = b.spans[...]
+    top = jnp.max(all_spans, 0)
+    whole_span = top + jnp.log(jnp.sum(jnp.exp(all_spans - top[None]), 0))
+    shared_in()
+
+    def lift(t):
+        rows = [pl.ds(h * TEAM + place, 1) for h in range(2)]
+        each = [jnp.exp(b.spans[t, rows[h], :] - b.flat[0, rows[h], :]) for h in range(2)]
+        return jnp.where(iota((128, ROWS), 0) < DH, each[0], each[1])
+
+    b.flat[0] = whole_span
+    acc = lift(place) * b.shared[place].astype(f32)
+    for j, (_, t) in enumerate(mates):
+        back = lax.rem(cy + 4 - (j // 2 + 1), 4) * 2 + (core if j % 2 == 0 else 1 - core)
+        acc = acc + lift(back if j < 6 else t) * b.shared_land[j].astype(f32)
+    b.context[...] = acc.T.astype(bf16)
+
+    b.attn[...] = nn(b.context[...], b.w_out[...]).astype(bf16)
+    attn_in = z_scatter(b.attn, b.attn_land)
+    factor = jnp.exp(span - stretch(b.flat, 0)) * scale
+
+    def norm_step(i, carry):
+        part = b.probs[chunk(i)] * factor
         b.probs[chunk(i)] = part
         b.probs_b[chunk(i)] = part.astype(bf16)
-        return acc + tn(b.vals[chunk(i)], part.astype(bf16))
-
-    acc = lax.fori_loop(0, KEYS // CHUNK, context_step, jnp.zeros((128, 256), f32))
-    tall = iota((128, 128), 0)
-    b.context[...] = jnp.where(tall < DH, acc[:, :128], acc[:, 128:]).T.astype(bf16)
-
-    b.attn[...] = nn(b.context[...], b.w_out[...]).astype(bf16)
-    attn_in = z_scatter(b.attn, b.attn_land)
+        return carry
+
+    lax.fori_loop(0, steps, norm_step, 0)
     attn_in()
     b.middle[own] = (b.tokens[own].astype(f32) + landed(b.attn, b.attn_land)).astype(bf16)
     middle_in = z_gather(b.middle)
@@ -478,7 +521,6 @@
     b.gmid[...] = nt(b.grad_pre[...], b.w_up[...]).astype(bf16)
     gmid_in = z_scatter(b.gmid, b.gmid_land)
     b.down[...] = nn(b.activated[...], b.w_down[...]).astype(bf16)
-    down_in = z_scatter(b.down, b.down_land)
     wg = {name: Reduce(name) for name in WEIGHT_GRADS}
     wg["down"].part[...] = tn(b.activated[...], b.cot[...]).astype(bf16)
     wg["down"].start()
@@ -491,78 +533,70 @@
     wg["down"].spread()
     grad_middle_in()
 
-    grad_context = nt(b.grad_middle[...], b.w_out[...]).astype(bf16)
-    lane = iota((ROWS, 128), 1)
-    b.d_two[pl.ds(0, ROWS)] = jnp.where(lane < DH, grad_context, zero)
-    b.d_two[pl.ds(ROWS, ROWS)] = jnp.where(lane < DH, zero, grad_context)
+    b.graded[place] = nt(b.grad_middle[...], b.w_out[...]).astype(bf16)
+    graded_in = team_gather(b.graded)
+    down_in = z_scatter(b.down, b.down_land)
+    row, lane5 = iota((128, 512), 0), iota((128, 512), 1)
+    total = jnp.zeros((512, 256), f32)
+    for q in range(4):
+        pick = (lane5 // 16 == row // 4) & (lax.rem(lane5, 16) == q * 4 + lax.rem(row, 4))
+        picked = nn(b.context[...], jnp.where(pick, 1.0, 0.0).astype(bf16)).astype(bf16)
+        total = total + tn(picked, b.grad_middle[:, q * 256 : (q + 1) * 256])
+    wg["out"].part[...] = total.astype(bf16)
+    graded_in()
+    two(b.d_two, lambda t: b.graded[t])
 
     def delta_step(i, total):
         part = nt(b.vals[chunk(i)], b.d_two[...])
         b.grad_probs[chunk(i)] = part
         return total + jnp.sum(eights(part * b.probs[chunk(i)]), 0)
 
-    delta = lax.fori_loop(0, KEYS // CHUNK, delta_step, jnp.zeros((8, 256), f32))
+    delta = lax.fori_loop(0, steps, delta_step, jnp.zeros((8, ASKED), f32))
     delta = jnp.sum(delta, 0, keepdims=True)
-
-    def back_step(i, acc):
-        grad = (b.probs[chunk(i)] * (b.grad_probs[chunk(i)] - delta)).astype(bf16)
-        b.gk[chunk(i)] = nn(grad, b.q_two[...]).astype(bf16)
-        b.gv[chunk(i)] = nn(b.probs_b[chunk(i)], b.d_two[...]).astype(bf16)
-        return acc + tn(b.keys[chunk(i)], grad)
-
-    halves = KEYS // CHUNK // 2
-    acc = lax.fori_loop(halves, 2 * halves, back_step, jnp.zeros((128, 256), f32))
-    kv_k = fresh(2)
-    send(b.gk.at[pl.ds(HALF, HALF)], b.gk_sib, kv_k, to_core(sib))
-    send(b.gv.at[pl.ds(HALF, HALF)], b.gv_sib, kv_k, to_core(sib))
-    pending.append((kv_k, b.gk))
-    acc = lax.fori_loop(0, halves, back_step, acc)
-    wait(rs.at[kv_k], b.gk)
-
-    def pair_step(i, carry):
-        rows = pl.ds(pl.multiple_of(i * ROWS, ROWS), ROWS)
-        b.gk_sum[i] = (b.gk[rows].astype(f32) + b.gk_sib[rows].astype(f32)).astype(bf16)
-        b.gv_sum[i] = (b.gv[rows].astype(f32) + b.gv_sib[rows].astype(f32)).astype(bf16)
+    for r in range(2 * TEAM):
+        b.deltas[place, pl.ds(r, 1), :] = delta[:, r * 128 : (r + 1) * 128]
+    deltas_in = team_gather(b.deltas)
+    for t in range(RING):
+        b.gv[t] = nn(b.probs_b[pl.ds(t * ROWS, ROWS)], b.d_two[...]).astype(bf16)
+    gv_in = ring_scatter(b.gv, b.gv_land)
+    deltas_in()
+    b.flat[1] = jnp.sum(b.deltas[...], 0)
+    delta = stretch(b.flat, 1)
+
+    def back_step(i, carry):
+        b.probs_b[chunk(i)] = (b.probs[chunk(i)] * (b.grad_probs[chunk(i)] - delta)).astype(bf16)
         return carry
 
-    lax.fori_loop(0, CHIPS, pair_step, 0)
-    for j, o in enumerate(offsets):
-        if j:
-            back = same_core(((4 - o[0]) % 4, (4 - o[1]) % 4))
-            send(b.gk_sum.at[j], b.gk_land.at[j - 1], kv_k + 1, back)
-            send(b.gv_sum.at[j], b.gv_land.at[j - 1], kv_k + 1, back)
-    both = b.gk.at[pl.ds(0, 2 * (CHIPS - 1) * ROWS)]
-    pending.append((kv_k + 1, both))
-
-    grad_query = jnp.where(tall < DH, acc[:, :128], acc[:, 128:]).T * DH ** (-0.5)
-    b.grad_rows[:, :128] = grad_query.astype(bf16)
+    lax.fori_loop(0, steps, back_step, 0)
+    for h in range(2):
+        side = slice(h * TEAM * ROWS, (h + 1) * TEAM * ROWS)
+        part = tn(b.keys[...], b.probs_b[:, side])
+        for t in range(TEAM):
+            b.gq[t, h * DH : (h + 1) * DH, :] = (
+                part[h * DH : (h + 1) * DH, t * ROWS : (t + 1) * ROWS].astype(bf16))
+    gq_in = team_scatter(b.gq, b.gq_land)
+    for t in range(RING):
+        b.gk[t] = nn(b.probs_b[pl.ds(t * ROWS, ROWS)], b.q_two[...]).astype(bf16)
+    gk_in = ring_scatter(b.gk, b.gk_land)
+
     down_in()
     b.layer[own] = (b.middle[own].astype(f32) + landed(b.down, b.down_land)).astype(bf16)
     layer_in = z_gather(b.layer)
+    wg["out"].start()
+    gdown_ref[...] = wg["down"].finish()
+    for c, part, land, come in ((2, b.gv, b.gv_land, gv_in), (0, b.gq, b.gq_land, gq_in), (1, b.gk, b.gk_land, gk_in)):
+        come()
+        total = part[cx if c else place].astype(f32)
+        for j in range(RING - 1 if c else TEAM - 1):
+            total = total + land[j].astype(f32)
+        if c == 0:
+            total = total.T * DH ** (-0.5)
+        b.grad_rows[:, c * 128 : (c + 1) * 128] = total.astype(bf16)
+
+    b.gin[...] = sum(nt(b.grad_rows[:, c * 128 : (c + 1) * 128], b.w_qkv[c]) for c in (1, 2, 0)).astype(bf16)
+    gin_in = z_scatter(b.gin, b.gin_land)
     wg["up"].spread()
-    row, lane = iota((128, 512), 0), iota((128, 512), 1)
-    total = jnp.zeros((512, 256), f32)
-    for q in range(4):
-        pick = (lane // 16 == row // 4) & (lax.rem(lane, 16) == q * 4 + lax.rem(row, 4))
-        picked = nn(b.context[...], jnp.where(pick, 1.0, 0.0).astype(bf16)).astype(bf16)
-        total = total + tn(picked, b.grad_middle[:, q * 256 : (q + 1) * 256])
-    wg["out"].part[...] = total.astype(bf16)
-    wg["out"].start()
-    layer_in()
-    layer_ref[...] = b.layer[...]
-    gdown_ref[...] = wg["down"].finish()
     wg["out"].spread()
-
-    wait(rs.at[kv_k + 1], both)
-    for c, part, other, land in ((1, b.gk, b.gk_sib, b.gk_land), (2, b.gv, b.gv_sib, b.gv_land)):
-        rows = pl.ds(0, ROWS)
-        total = part[rows].astype(f32) + other[rows].astype(f32)
-        for j in range(CHIPS - 1):
-            total = total + land[j].astype(f32)
-        b.grad_rows[:, c * 128 : (c + 1) * 128] = total.astype(bf16)
-
-    b.gin[...] = nt(b.grad_rows[...], b.w_qkv[...]).astype(bf16)
-    gin_in = z_scatter(b.gin, b.gin_land)
     wg["qkv"].part[...] = tn(b.normed_in[...], b.grad_rows[...]).astype(bf16)
     wg["qkv"].start()
     wg["qkv"].spread()
@@ -576,11 +610,18 @@
         gout_ref[:, q * 256 : (q + 1) * 256] = total[q * 4 : (q + 1) * 4]
     total = wg["qkv"].finish()
     for c in range(3):
-        gqkv_ref[:, c, :] = total[:, c * 128 : (c + 1) * 128]
+        gqkv_ref[c] = total[:, c * 128 : (c + 1) * 128]
     grad_tok_in()
     gtok_ref[...] = b.grad_tok[...]
+    layer_in()
+    layer_ref[...] = b.layer[...]
     for k, ref in pending:
         wait(ss.at[k], ref)
+
+
+def hand_over(*refs):
+    for i in range(6):
+        refs[6 + i][...] = refs[i][...]
 
 
 def shards(pixels, valid_mask, var_ids, embed_weight, var_table, agg_query, agg_key,
@@ -589,11 +630,11 @@
     in_smem = pl.BlockSpec(memory_space=pltpu.SMEM)
     anywhere = pl.BlockSpec(memory_space=pl.ANY)
     big = (agg_key, pixels, embed_weight, var_table, agg_value, agg_out, pos_embed,
-           w_qkv.reshape(D, 384), w_out, w_up, w_down, cotangent)
+           w_qkv.transpose(1, 0, 2), w_out, w_up, w_down, cotangent)
     shape = jax.ShapeDtypeStruct
-    return tuple(pl.pallas_call(
+    outs = pl.pallas_call(
         whole_kernel,
-        out_shape=[shape((ROWS, D), bf16), shape((ROWS, D), bf16), shape((32, 3, 128), f32),
+        out_shape=[shape((ROWS, D), bf16), shape((ROWS, D), bf16), shape((3, 32, 128), f32),
                    shape((4, D), f32), shape((32, HID), f32), shape((16, D), f32)],
         in_specs=[in_smem, in_smem, in_vmem] + [anywhere] * len(big),
         out_specs=[in_vmem] * 6,
@@ -603,7 +644,15 @@
         compiler_params=pltpu.CompilerParams(
             collective_id=0, has_side_effects=True, vmem_limit_bytes=60 * 2**20),
         name="whole",
-    )(valid_mask, var_ids, agg_query.reshape(1, D), *big))
+    )(valid_mask, var_ids, agg_query.reshape(1, D), *big)
+    layer_out, grad_tokens, grad_qkv, grad_out, grad_up, grad_down = pl.pallas_call(
+        hand_over,
+        out_shape=[shape(x.shape, x.dtype) for x in outs],
+        in_specs=[in_vmem] * 6,
+        out_specs=[in_vmem] * 6,
+        name="hand_over",
+    )(*outs)
+    return (layer_out, grad_tokens, grad_qkv.transpose(1, 0, 2), grad_out, grad_up, grad_down)
 
 
 def solution(mesh):

time: 149 us -> 125 us (0.84)
  the two profiles are of different devices: /device:TPU:3 before, /device:TPU:1 now
where the time goes in v3:
time: 125 us
  Pallas kernels  125 us (100%)
    pallas_call x1, Pallas kernels, shards(): pl.pallas_call(whole_kernel, out_shape=[shape((ROWS, D), bf16), shape((RO...  123 us

profile of v3, /device:TPU:1, one launch (start us, length us, event | category | flops | bytes accessed | tf_op | source)
XLA Modules:
  0.0 125.2 jit_solution(12199021154308369247)
XLA Ops:
  0.6 122.7 %whole.1 = (bf16[128,1024]{1,0:T(8,128)(2,1)}, bf16[128,1024]{1,0:T(8,128)(2,1)}, f32[3,32,128]{2,1,0:T(8,128)}, f32[4,1024]{1,0:T(4,128)}, f32[32,512]{1,0:T(8,128)}, /*index=5*/f32[16,1024]{1,0:T(8,128)}) custom-call(s32[12]{0:T(128)} %refs_0_.1, s32[12]{0:T(128)} %refs_1_.1, f32[1,1024]{1,0:T(1,128)} %bitcast.4, bf16[32,1024]{1,0:T(8,128)(2,1)} %refs_3_.1, ...), custom_call_target="tpu_custom_call" | custom-call | tf_op jit(solution)/shard_map/whole/pallas_call | solution.py:635
  123.3 1.9 %hand_over.1 = (bf16[128,1024]{1,0:T(8,128)(2,1)}, bf16[128,1024]{1,0:T(8,128)(2,1)}, f32[3,32,128]{2,1,0:T(8,128)}, f32[4,1024]{1,0:T(4,128)}, f32[32,512]{1,0:T(8,128)}, /*index=5*/f32[16,1024]{1,0:T(8,128)}) custom-call(bf16[128,1024]{1,0:T(8,128)(2,1)} %get-tuple-element.18.refs_0_, bf16[128,1024]{1,0:T(8,128)(2,1)} %get-tuple-element.19.refs_1_, ...), custom_call_target="tpu_custom_call" | custom-call | tf_op jit(solution)/shard_map/hand_over/pallas_call | solution.py:648

commit v4 on v3

--- a/solution.py
+++ b/solution.py
@@ -94,7 +94,10 @@
     shares=((SLOTS * ROWS, 128), bf16),
     pooled=((ROWS, D), bf16),
     level=((ROWS, 128), f32),
-    pooled_land=((7, PART, D), bf16),
+    pooled_land=((2, 7, PART, D // 2), bf16),
+    mixed=((ROWS, D), bf16),
+    w_full=((NV, RING, 2, PART, D), bf16),
+    context_all=((NV, ROWS, 128), bf16),
     level_land=((7, PART, 128), f32),
     tokens=((ROWS, D), bf16),
     normed_in=((ROWS, D), bf16),
@@ -113,15 +116,14 @@
     shared=((TEAM, 128, ROWS), bf16),
     shared_land=((TEAM, 128, ROWS), bf16),
     context=((ROWS, 128), bf16),
-    attn=((ROWS, D), bf16),
-    attn_land=((7, PART, D), bf16),
     middle=((ROWS, D), bf16),
     normed_mid=((ROWS, D), bf16),
     upstream=((ROWS, HID), f32),
     activated=((ROWS, HID), bf16),
     grad_pre=((ROWS, HID), bf16),
     gmid=((ROWS, D), bf16),
-    gmid_land=((7, PART, D), bf16),
+    gmid_land=((2, 7, PART, D // 2), bf16),
+    gmid_sum=((ROWS, D), bf16),
     down=((ROWS, D), bf16),
     down_land=((7, PART, D), bf16),
     layer=((ROWS, D), bf16),
@@ -134,8 +136,8 @@
     gv_land=((RING - 1, ROWS, 128), bf16),
     grad_rows=((ROWS, 384), bf16),
     gin=((ROWS, D), bf16),
-    gin_land=((7, PART, D), bf16),
-    grad_tok=((ROWS, D), bf16),
+    gin_land=((2, 7, PART, D // 2), bf16),
+    gin_sum=((ROWS, D), bf16),
 )
 WEIGHT_GRADS = dict(down=(16, D), up=(32, HID), out=(16, 256), qkv=(32, 384))
 for _name, (_r, _w) in WEIGHT_GRADS.items():
@@ -143,9 +145,9 @@
     SCRATCH["wg_sib_" + _name] = ((CHIPS, _r, _w), bf16)
     SCRATCH["wg_sum_" + _name] = ((CHIPS, _r, _w), bf16)
     SCRATCH["wg_land_" + _name] = ((CHIPS - 1, _r, _w), bf16)
-LOADED = ("agg_key", "pixels", "embed_w", "table", "agg_value", "agg_out", "pos", "w_qkv",
-          "w_out", "w_up", "w_down", "cot")
-SEMS = 160
+LOADED = ("agg_key", "w_out", "table", "pixels", "embed_w", "agg_value", "w_down", "cot", "agg_out",
+          "pos", "w_qkv", "w_up")
+SEMS = 128
 
 
 class Names:
@@ -233,6 +235,40 @@
             send(ref.at[own], ref.at[own], k, {"var": lax.rem(v + d, NV)})
         pending.append((k, ref.at[pl.ds(0, 7 * PART)]))
         return lambda: wait(rs.at[k], ref.at[pl.ds(0, 7 * PART)])
+
+    class Halves:
+        def __init__(self, src, land, out):
+            self.src, self.land, self.out = src, land, out
+            self.k = fresh(4)
+
+        def columns(self, half):
+            return pl.ds(half * (D // 2), D // 2)
+
+        def start(self, half):
+            for d in FAR_FIRST:
+                there = lax.rem(v + d, NV)
+                send(self.src.at[pl.ds(pl.multiple_of(there * PART, PART), PART), self.columns(half)],
+                     self.land.at[half, d - 1], self.k + half, {"var": there})
+            pending.append((self.k + half, self.land.at[half]))
+
+        def turn(self, half, add=None):
+            wait(rs.at[self.k + half], self.land.at[half])
+            parts = [self.src[own, self.columns(half)]] + [self.land[half, d] for d in range(7)]
+            if add is None:
+                total = parts[0].astype(f32)
+                for part in parts[1:]:
+                    total = total + part.astype(f32)
+            else:
+                total = add(parts)
+            self.out[own, self.columns(half)] = total.astype(bf16)
+            for d in FAR_FIRST:
+                send(self.out.at[own, self.columns(half)], self.out.at[own, self.columns(half)],
+                     self.k + 2 + half, {"var": lax.rem(v + d, NV)})
+            pending.append((self.k + 2 + half, self.land.at[half]))
+
+        def finish(self):
+            for half in range(2):
+                wait(rs.at[self.k + 2 + half], self.land.at[half])
 
     def landed(src, land):
         total = src[own].astype(f32)
@@ -336,6 +372,18 @@
         send(b.dirs_part, b.dirs_land.at[0, j + 1], dirs_k, same_core(o))
     pending.append((dirs_k, b.dirs_land.at[0, pl.ds(1, CHIPS - 1)]))
 
+    ready("w_out")
+    columns = pl.ds(pl.multiple_of(cx * 256, 256), 256)
+    piece = pl.ds(pl.multiple_of(place * PART, PART), PART)
+    full_k = fresh(CHIPS + 1)
+    for d in FAR_FIRST:
+        send(b.w_out.at[piece, columns], b.w_full.at[v, cy, core, :, columns], full_k,
+             {"var": lax.rem(v + d, NV)})
+    b.w_full[v, cy, core, :, columns] = b.w_out[piece, columns]
+    seven = b.w_full.at[pl.ds(0, NV - 1), 0, 0, :, pl.ds(0, 256)]
+    eight = b.w_full.at[:, 0, 0, :, pl.ds(0, 256)]
+    pending.append((full_k, seven))
+
     ready("table")
     row, lane = iota((16, V), 0), iota((16, V), 1)
     picks = jnp.zeros((16, V), f32)
@@ -354,6 +402,11 @@
     wait(rs.at[dirs_k], b.dirs_land.at[0, pl.ds(1, CHIPS - 1)])
     send(b.dirs_land.at[0], b.dirs_land.at[1], dirs_k + 1, to_core(sib))
     pending.append((dirs_k + 1, b.dirs_land.at[1]))
+    wait(rs.at[full_k], seven)
+    for j, o in enumerate(offsets[1:]):
+        send(b.w_full.at[:, cy, core, :, columns], b.w_full.at[:, cy, core, :, columns],
+             full_k + 1 + j, same_core(o))
+        pending.append((full_k + 1 + j, eight))
     ready("agg_value")
 
     def value_columns(i, carry):
@@ -389,15 +442,17 @@
     for i in range(SLOTS):
         rows = pl.ds(i * ROWS, ROWS)
         b.shares[rows] = thirds(b.scores[rows] * scale, lane)
+    level_in = z_scatter(b.level, b.level_land)
+    pooled = Halves(b.pooled, b.pooled_land, b.mixed)
     for c in range(4):
         columns = slice(c * 256, (c + 1) * 256)
+        wide = nn(b.shares[...], spread_one[:, columns])
         acc = jnp.zeros((ROWS, 256), f32)
         for i in range(SLOTS):
-            rows = pl.ds(i * ROWS, ROWS)
-            acc = acc + nn(b.shares[rows], spread_one[:, columns]) * b.values[rows, columns]
+            acc = acc + wide[i * ROWS : (i + 1) * ROWS] * b.values[pl.ds(i * ROWS, ROWS), columns]
         b.pooled[:, columns] = acc.astype(bf16)
-    level_in = z_scatter(b.level, b.level_land)
-    pooled_in = z_scatter(b.pooled, b.pooled_land)
+        if c % 2:
+            pooled.start(c // 2)
 
     ready("w_down", "cot")
     b.upstream[...] = nt(b.cot[...], b.w_down[...])
@@ -409,14 +464,17 @@
     scale = 1.0 / sum(lifts[1:], lifts[0])
     lane = iota((PART, 128), 1)
     lifts = [nn(thirds(x * scale, lane), spread_one) for x in lifts]
-    pooled_in()
-    mixed = lifts[0] * b.pooled[own].astype(f32)
-    for d in range(7):
-        mixed = mixed + lifts[d + 1] * b.pooled_land[d].astype(f32)
-    b.tokens[own] = (nn(mixed.astype(bf16), b.agg_out[...]) + b.pos[own].astype(f32)).astype(bf16)
-    tokens_in = z_gather(b.tokens)
-    ready("w_qkv", "w_out", "w_up")
-    tokens_in()
+    half = D // 2
+    for h in range(2):
+        pooled.turn(h, lambda parts: sum(
+            lifts[i][:, h * half : (h + 1) * half] * parts[i].astype(f32) for i in range(NV)))
+    for j in range(CHIPS - 1):
+        wait(rs.at[full_k + 1 + j], eight)
+    send(b.w_full.at[:, :, core], b.w_full.at[:, :, core], full_k + CHIPS, to_core(sib))
+    pending.append((full_k + CHIPS, b.w_full.at[:, :, 0]))
+    ready("w_qkv", "w_up")
+    pooled.finish()
+    b.tokens[...] = (nn(b.mixed[...], b.agg_out[...]) + b.pos[...].astype(f32)).astype(bf16)
 
     b.normed_in[...] = layer_norm(b.tokens[...]).astype(bf16)
     mine = pl.ds(pl.multiple_of(cx * ROWS, ROWS), ROWS)
@@ -495,9 +553,13 @@
         back = lax.rem(cy + 4 - (j // 2 + 1), 4) * 2 + (core if j % 2 == 0 else 1 - core)
         acc = acc + lift(back if j < 6 else t) * b.shared_land[j].astype(f32)
     b.context[...] = acc.T.astype(bf16)
-
-    b.attn[...] = nn(b.context[...], b.w_out[...]).astype(bf16)
-    attn_in = z_scatter(b.attn, b.attn_land)
+    b.context_all[v] = b.context[...]
+
+    k = fresh()
+    seven = b.context_all.at[pl.ds(0, NV - 1)]
+    for d in FAR_FIRST:
+        send(b.context_all.at[v], b.context_all.at[v], k, {"var": lax.rem(v + d, NV)})
+    pending.append((k, seven))
     factor = jnp.exp(span - stretch(b.flat, 0)) * scale
 
     def norm_step(i, carry):
@@ -507,10 +569,11 @@
         return carry
 
     lax.fori_loop(0, steps, norm_step, 0)
-    attn_in()
-    b.middle[own] = (b.tokens[own].astype(f32) + landed(b.attn, b.attn_land)).astype(bf16)
-    middle_in = z_gather(b.middle)
-    middle_in()
+    wait(rs.at[full_k + CHIPS], b.w_full.at[:, :, 0])
+    wait(rs.at[k], seven)
+    all_context = jnp.concatenate([b.context_all[i] for i in range(NV)], 1)
+    b.middle[...] = (b.tokens[...].astype(f32)
+                     + nn(all_context, b.w_full[...].reshape(D, D))).astype(bf16)
 
     b.normed_mid[...] = layer_norm(b.middle[...]).astype(bf16)
     pre = nn(b.normed_mid[...], b.w_up[...])
@@ -518,20 +581,23 @@
     b.activated[...] = (pre * half).astype(bf16)
     slope = half + pre * (jnp.exp(-0.5 * pre * pre) * 0.3989422804014327)
     b.grad_pre[...] = (b.upstream[...] * slope).astype(bf16)
-    b.gmid[...] = nt(b.grad_pre[...], b.w_up[...]).astype(bf16)
-    gmid_in = z_scatter(b.gmid, b.gmid_land)
+    gmid = Halves(b.gmid, b.gmid_land, b.gmid_sum)
+    for h in range(2):
+        half = pl.ds(h * (D // 2), D // 2)
+        b.gmid[:, half] = nt(b.grad_pre[...], b.w_up[half]).astype(bf16)
+        gmid.start(h)
     b.down[...] = nn(b.activated[...], b.w_down[...]).astype(bf16)
     wg = {name: Reduce(name) for name in WEIGHT_GRADS}
     wg["down"].part[...] = tn(b.activated[...], b.cot[...]).astype(bf16)
     wg["down"].start()
-    gmid_in()
-    b.grad_middle[own] = (b.cot[own].astype(f32) + norm_back(
-        b.middle[own], landed(b.gmid, b.gmid_land))).astype(bf16)
-    grad_middle_in = z_gather(b.grad_middle)
+    gmid.turn(0)
+    gmid.turn(1)
     wg["up"].part[...] = tn(b.normed_mid[...], b.grad_pre[...]).astype(bf16)
     wg["up"].start()
     wg["down"].spread()
-    grad_middle_in()
+    gmid.finish()
+    b.grad_middle[...] = (b.cot[...].astype(f32) + norm_back(
+        b.middle[...], b.gmid_sum[...].astype(f32))).astype(bf16)
 
     b.graded[place] = nt(b.grad_middle[...], b.w_out[...]).astype(bf16)
     graded_in = team_gather(b.graded)
@@ -593,17 +659,19 @@
             total = total.T * DH ** (-0.5)
         b.grad_rows[:, c * 128 : (c + 1) * 128] = total.astype(bf16)
 
-    b.gin[...] = sum(nt(b.grad_rows[:, c * 128 : (c + 1) * 128], b.w_qkv[c]) for c in (1, 2, 0)).astype(bf16)
-    gin_in = z_scatter(b.gin, b.gin_land)
+    gin = Halves(b.gin, b.gin_land, b.gin_sum)
+    for h in range(2):
+        half = pl.ds(h * (D // 2), D // 2)
+        b.gin[:, half] = sum(
+            nt(b.grad_rows[:, c * 128 : (c + 1) * 128], b.w_qkv[c, half]) for c in (1, 2, 0)).astype(bf16)
+        gin.start(h)
     wg["up"].spread()
     wg["out"].spread()
     wg["qkv"].part[...] = tn(b.normed_in[...], b.grad_rows[...]).astype(bf16)
     wg["qkv"].start()
     wg["qkv"].spread()
-    gin_in()
-    b.grad_tok[own] = (b.grad_middle[own].astype(f32) + norm_back(
-        b.tokens[own], landed(b.gin, b.gin_land))).astype(bf16)
-    grad_tok_in = z_gather(b.grad_tok)
+    gin.turn(0)
+    gin.turn(1)
     gup_ref[...] = wg["up"].finish()
     total = wg["out"].finish()
     for q in range(4):
@@ -611,8 +679,9 @@
     total = wg["qkv"].finish()
     for c in range(3):
         gqkv_ref[c] = total[:, c * 128 : (c + 1) * 128]
-    grad_tok_in()
-    gtok_ref[...] = b.grad_tok[...]
+    gin.finish()
+    gtok_ref[...] = (b.grad_middle[...].astype(f32) + norm_back(
+        b.tokens[...], b.gin_sum[...].astype(f32))).astype(bf16)
     layer_in()
     layer_ref[...] = b.layer[...]
     for k, ref in pending:
@@ -629,8 +698,8 @@
     in_vmem = pl.BlockSpec(memory_space=pltpu.VMEM)
     in_smem = pl.BlockSpec(memory_space=pltpu.SMEM)
     anywhere = pl.BlockSpec(memory_space=pl.ANY)
-    big = (agg_key, pixels, embed_weight, var_table, agg_value, agg_out, pos_embed,
-           w_qkv.transpose(1, 0, 2), w_out, w_up, w_down, cotangent)
+    big = (agg_key, w_out, var_table, pixels, embed_weight, agg_value, w_down, cotangent, agg_out,
+           pos_embed, w_qkv.transpose(1, 0, 2), w_up)
     shape = jax.ShapeDtypeStruct
     outs = pl.pallas_call(
         whole_kernel,

time: 125 us -> 114 us (0.912)
  Pallas kernels: 125 us -> 113 us
    pallas_call x1, Pallas kernels: 123 us -> 111 us  [shards(): pl.pallas_call(whole_kernel, out_shape=[shape((ROWS, D), bf16), shape((RO...]
where the time goes in v4:
time: 114 us
  Pallas kernels  113 us (99%)
    pallas_call x1, Pallas kernels, shards(): pl.pallas_call(whole_kernel, out_shape=[shape((ROWS, D), bf16), shape((RO...  111 us

profile of v4, /device:TPU:1, one launch (start us, length us, event | category | flops | bytes accessed | tf_op | source)
XLA Modules:
  0.0 113.9 jit_solution(4723001900358015201)
XLA Ops:
  0.6 111.3 %whole.1 = (bf16[128,1024]{1,0:T(8,128)(2,1)}, bf16[128,1024]{1,0:T(8,128)(2,1)}, f32[3,32,128]{2,1,0:T(8,128)}, f32[4,1024]{1,0:T(4,128)}, f32[32,512]{1,0:T(8,128)}, /*index=5*/f32[16,1024]{1,0:T(8,128)}) custom-call(s32[12]{0:T(128)} %refs_0_.1, s32[12]{0:T(128)} %refs_1_.1, f32[1,1024]{1,0:T(1,128)} %bitcast.4, bf16[32,1024]{1,0:T(8,128)(2,1)} %refs_3_.1, ...), custom_call_target="tpu_custom_call" | custom-call | tf_op jit(solution)/shard_map/whole/pallas_call | solution.py:704
  112.0 1.9 %hand_over.1 = (bf16[128,1024]{1,0:T(8,128)(2,1)}, bf16[128,1024]{1,0:T(8,128)(2,1)}, f32[3,32,128]{2,1,0:T(8,128)}, f32[4,1024]{1,0:T(4,128)}, f32[32,512]{1,0:T(8,128)}, /*index=5*/f32[16,1024]{1,0:T(8,128)}) custom-call(bf16[128,1024]{1,0:T(8,128)(2,1)} %get-tuple-element.18.refs_0_, bf16[128,1024]{1,0:T(8,128)(2,1)} %get-tuple-element.19.refs_1_, ...), custom_call_target="tpu_custom_call" | custom-call | tf_op jit(solution)/shard_map/hand_over/pallas_call | solution.py:717

commit v5 on v4

--- a/solution.py
+++ b/solution.py
@@ -109,9 +109,13 @@
     d_two=((ASKED, 128), bf16),
     probs=((KEYS, ASKED), f32),
     probs_b=((KEYS, ASKED), bf16),
-    grad_probs=((KEYS, ASKED), f32),
+    low_b=((KEYS, ASKED), bf16),
+    part_keep=((TEAM, 128, ROWS), f32),
+    low=((TEAM, 128, ROWS), bf16),
+    low_land=((TEAM, 128, ROWS), bf16),
+    exact=((128, ROWS), f32),
     spans=((TEAM, 2 * TEAM, 128), f32),
-    deltas=((TEAM, 2 * TEAM, 128), f32),
+    deltas=((TEAM, 8, 128), f32),
     flat=((2, 2 * TEAM, 128), f32),
     shared=((TEAM, 128, ROWS), bf16),
     shared_land=((TEAM, 128, ROWS), bf16),
@@ -145,8 +149,9 @@
     SCRATCH["wg_sib_" + _name] = ((CHIPS, _r, _w), bf16)
     SCRATCH["wg_sum_" + _name] = ((CHIPS, _r, _w), bf16)
     SCRATCH["wg_land_" + _name] = ((CHIPS - 1, _r, _w), bf16)
-LOADED = ("agg_key", "w_out", "table", "pixels", "embed_w", "agg_value", "w_down", "cot", "agg_out",
+LOADED = ("agg_key", "table", "pixels", "embed_w", "w_out", "agg_value", "w_down", "cot", "agg_out",
           "pos", "w_qkv", "w_up")
+EARLY = 4
 SEMS = 128
 
 
@@ -205,7 +210,8 @@
     loads = {}
     for i, name in enumerate(LOADED):
         loads[name] = pltpu.make_async_copy(hbm[name], getattr(b, name), load_sem.at[i])
-        loads[name].start()
+        if i < EARLY:
+            loads[name].start()
 
     def ready(*names):
         for name in names:
@@ -366,6 +372,23 @@
     b.dirs_part[...] = dirs.astype(bf16)
     b.dirs_land[0, 0] = dirs.astype(bf16)
 
+    ready("table")
+    row, lane = iota((16, V), 0), iota((16, V), 1)
+    picks = jnp.zeros((16, V), f32)
+    for i in range(SLOTS):
+        picks = picks + jnp.where((row == i) & (lane == ids_ref[i]), 1.0, 0.0)
+    b.table_rows[...] = nn(picks.astype(bf16), b.table[...])
+    ready("pixels", "embed_w")
+    for name in LOADED[EARLY:]:
+        loads[name].start()
+
+    def embed(i, carry):
+        raw = tn(b.pixels[i], b.embed_w[i])
+        b.embedded[pl.ds(pl.multiple_of(i * ROWS, ROWS), ROWS)] = (
+            raw + b.table_rows[pl.ds(i, 1)]).astype(bf16)
+        return carry
+
+    lax.fori_loop(0, SLOTS, embed, 0, unroll=3)
     pl.semaphore_wait(barrier, 7 + CHIPS - 1 + 1 + RING - 1)
     dirs_k = fresh(2)
     for j, o in enumerate(offsets[1:]):
@@ -384,21 +407,17 @@
     eight = b.w_full.at[:, 0, 0, :, pl.ds(0, 256)]
     pending.append((full_k, seven))
 
-    ready("table")
-    row, lane = iota((16, V), 0), iota((16, V), 1)
-    picks = jnp.zeros((16, V), f32)
-    for i in range(SLOTS):
-        picks = picks + jnp.where((row == i) & (lane == ids_ref[i]), 1.0, 0.0)
-    b.table_rows[...] = nn(picks.astype(bf16), b.table[...])
-    ready("pixels", "embed_w")
-
-    def embed(i, carry):
-        raw = tn(b.pixels[i], b.embed_w[i])
-        b.embedded[pl.ds(pl.multiple_of(i * ROWS, ROWS), ROWS)] = (
-            raw + b.table_rows[pl.ds(i, 1)]).astype(bf16)
+
+    ready("agg_value")
+
+    def value_columns(i, carry):
+        columns = pl.ds(pl.multiple_of(i * 256, 256), 256)
+        for m in range(2):
+            these = pl.ds(m * 768, 768)
+            b.values[these, columns] = nn(b.embedded[these], b.agg_value[:, columns])
         return carry
 
-    lax.fori_loop(0, SLOTS, embed, 0)
+    lax.fori_loop(0, 3, value_columns, 0)
     wait(rs.at[dirs_k], b.dirs_land.at[0, pl.ds(1, CHIPS - 1)])
     send(b.dirs_land.at[0], b.dirs_land.at[1], dirs_k + 1, to_core(sib))
     pending.append((dirs_k + 1, b.dirs_land.at[1]))
@@ -407,16 +426,7 @@
         send(b.w_full.at[:, cy, core, :, columns], b.w_full.at[:, cy, core, :, columns],
              full_k + 1 + j, same_core(o))
         pending.append((full_k + 1 + j, eight))
-    ready("agg_value")
-
-    def value_columns(i, carry):
-        columns = pl.ds(pl.multiple_of(i * 256, 256), 256)
-        for m in range(2):
-            these = pl.ds(m * 768, 768)
-            b.values[these, columns] = nn(b.embedded[these], b.agg_value[:, columns])
-        return carry
-
-    lax.fori_loop(0, 4, value_columns, 0)
+    value_columns(3, 0)
     wait(rs.at[dirs_k + 1], b.dirs_land.at[1])
     for j, o in enumerate(offsets):
         source = lax.rem(cx - o[0] + 4, 4) * 4 + lax.rem(cy - o[1] + 4, 4)
@@ -533,9 +543,24 @@
         side = slice(h * TEAM * ROWS, (h + 1) * TEAM * ROWS)
         part = tn(b.vals[...], b.probs_b[:, side]) * scale[:, side]
         for t in range(TEAM):
-            b.shared[t, h * DH : (h + 1) * DH, :] = (
-                part[h * DH : (h + 1) * DH, t * ROWS : (t + 1) * ROWS].astype(bf16))
+            here = part[h * DH : (h + 1) * DH, t * ROWS : (t + 1) * ROWS]
+            b.part_keep[t, h * DH : (h + 1) * DH, :] = here
+            b.shared[t, h * DH : (h + 1) * DH, :] = here.astype(bf16)
     shared_in = team_scatter(b.shared, b.shared_land)
+
+    def low_step(i, carry):
+        b.low_b[chunk(i)] = (b.probs[chunk(i)] - b.probs_b[chunk(i)].astype(f32)).astype(bf16)
+        return carry
+
+    lax.fori_loop(0, steps, low_step, 0)
+    for h in range(2):
+        side = slice(h * TEAM * ROWS, (h + 1) * TEAM * ROWS)
+        part = tn(b.vals[...], b.low_b[:, side]) * scale[:, side]
+        rows = slice(h * DH, (h + 1) * DH)
+        for t in range(TEAM):
+            b.low[t, rows, :] = (part[rows, t * ROWS : (t + 1) * ROWS] + (
+                b.part_keep[t, rows, :] - b.shared[t, rows, :].astype(f32))).astype(bf16)
+    low_in = team_scatter(b.low, b.low_land)
     spans_in()
     all_spans = b.spans[...]
     top = jnp.max(all_spans, 0)
@@ -548,10 +573,12 @@
         return jnp.where(iota((128, ROWS), 0) < DH, each[0], each[1])
 
     b.flat[0] = whole_span
-    acc = lift(place) * b.shared[place].astype(f32)
+    lifted = [lift(place)]
+    acc = lifted[0] * b.shared[place].astype(f32)
     for j, (_, t) in enumerate(mates):
         back = lax.rem(cy + 4 - (j // 2 + 1), 4) * 2 + (core if j % 2 == 0 else 1 - core)
-        acc = acc + lift(back if j < 6 else t) * b.shared_land[j].astype(f32)
+        lifted.append(lift(back if j < 6 else t))
+        acc = acc + lifted[-1] * b.shared_land[j].astype(f32)
     b.context[...] = acc.T.astype(bf16)
     b.context_all[v] = b.context[...]
 
@@ -569,6 +596,11 @@
         return carry
 
     lax.fori_loop(0, steps, norm_step, 0)
+    low_in()
+    acc = acc + lifted[0] * b.low[place].astype(f32)
+    for j in range(TEAM - 1):
+        acc = acc + lifted[j + 1] * b.low_land[j].astype(f32)
+    b.exact[...] = acc
     wait(rs.at[full_k + CHIPS], b.w_full.at[:, :, 0])
     wait(rs.at[k], seven)
     all_context = jnp.concatenate([b.context_all[i] for i in range(NV)], 1)
@@ -601,6 +633,11 @@
 
     b.graded[place] = nt(b.grad_middle[...], b.w_out[...]).astype(bf16)
     graded_in = team_gather(b.graded)
+    products = b.graded[place].astype(f32).T * b.exact[...]
+    b.deltas[place] = jnp.zeros((8, 128), f32)
+    for h in range(2):
+        b.deltas[place, pl.ds(h, 1), :] = jnp.sum(products[h * DH : (h + 1) * DH], 0, keepdims=True)
+    deltas_in = team_gather(b.deltas)
     down_in = z_scatter(b.down, b.down_land)
     row, lane5 = iota((128, 512), 0), iota((128, 512), 1)
     total = jnp.zeros((512, 256), f32)
@@ -609,28 +646,20 @@
         picked = nn(b.context[...], jnp.where(pick, 1.0, 0.0).astype(bf16)).astype(bf16)
         total = total + tn(picked, b.grad_middle[:, q * 256 : (q + 1) * 256])
     wg["out"].part[...] = total.astype(bf16)
+    wg["out"].start()
     graded_in()
     two(b.d_two, lambda t: b.graded[t])
 
-    def delta_step(i, total):
-        part = nt(b.vals[chunk(i)], b.d_two[...])
-        b.grad_probs[chunk(i)] = part
-        return total + jnp.sum(eights(part * b.probs[chunk(i)]), 0)
-
-    delta = lax.fori_loop(0, steps, delta_step, jnp.zeros((8, ASKED), f32))
-    delta = jnp.sum(delta, 0, keepdims=True)
-    for r in range(2 * TEAM):
-        b.deltas[place, pl.ds(r, 1), :] = delta[:, r * 128 : (r + 1) * 128]
-    deltas_in = team_gather(b.deltas)
     for t in range(RING):
         b.gv[t] = nn(b.probs_b[pl.ds(t * ROWS, ROWS)], b.d_two[...]).astype(bf16)
     gv_in = ring_scatter(b.gv, b.gv_land)
     deltas_in()
-    b.flat[1] = jnp.sum(b.deltas[...], 0)
-    delta = stretch(b.flat, 1)
+    delta = jnp.concatenate(
+        [b.deltas[t, pl.ds(h, 1), :] for h in range(2) for t in range(TEAM)], 1)
 
     def back_step(i, carry):
-        b.probs_b[chunk(i)] = (b.probs[chunk(i)] * (b.grad_probs[chunk(i)] - delta)).astype(bf16)
+        part = nt(b.vals[chunk(i)], b.d_two[...])
+        b.probs_b[chunk(i)] = (b.probs[chunk(i)] * (part - delta)).astype(bf16)
         return carry
 
     lax.fori_loop(0, steps, back_step, 0)
@@ -648,8 +677,8 @@
     down_in()
     b.layer[own] = (b.middle[own].astype(f32) + landed(b.down, b.down_land)).astype(bf16)
     layer_in = z_gather(b.layer)
-    wg["out"].start()
-    gdown_ref[...] = wg["down"].finish()
+    wg["up"].spread()
+    wg["out"].spread()
     for c, part, land, come in ((2, b.gv, b.gv_land, gv_in), (0, b.gq, b.gq_land, gq_in), (1, b.gk, b.gk_land, gk_in)):
         come()
         total = part[cx if c else place].astype(f32)
@@ -665,10 +694,9 @@
         b.gin[:, half] = sum(
             nt(b.grad_rows[:, c * 128 : (c + 1) * 128], b.w_qkv[c, half]) for c in (1, 2, 0)).astype(bf16)
         gin.start(h)
-    wg["up"].spread()
-    wg["out"].spread()
     wg["qkv"].part[...] = tn(b.normed_in[...], b.grad_rows[...]).astype(bf16)
     wg["qkv"].start()
+    gdown_ref[...] = wg["down"].finish()
     wg["qkv"].spread()
     gin.turn(0)
     gin.turn(1)
@@ -698,7 +726,7 @@
     in_vmem = pl.BlockSpec(memory_space=pltpu.VMEM)
     in_smem = pl.BlockSpec(memory_space=pltpu.SMEM)
     anywhere = pl.BlockSpec(memory_space=pl.ANY)
-    big = (agg_key, w_out, var_table, pixels, embed_weight, agg_value, w_down, cotangent, agg_out,
+    big = (agg_key, var_table, pixels, embed_weight, w_out, agg_value, w_down, cotangent, agg_out,
            pos_embed, w_qkv.transpose(1, 0, 2), w_up)
     shape = jax.ShapeDtypeStruct
     outs = pl.pallas_call(

time: 114 us -> 110 us (0.965)
  Pallas kernels: 113 us -> 109 us
    pallas_call x1, Pallas kernels: 111 us -> 107 us  [shards(): pl.pallas_call(whole_kernel, out_shape=[shape((ROWS, D), bf16), shape((RO...]
where the time goes in v5:
time: 110 us
  Pallas kernels  109 us (99%)
    pallas_call x1, Pallas kernels, shards(): pl.pallas_call(whole_kernel, out_shape=[shape((ROWS, D), bf16), shape((RO...  107 us

profile of v5, /device:TPU:1, one launch (start us, length us, event | category | flops | bytes accessed | tf_op | source)
XLA Modules:
  0.0 109.9 jit_solution(17730113496913073532)
XLA Ops:
  0.6 107.3 %whole.1 = (bf16[128,1024]{1,0:T(8,128)(2,1)}, bf16[128,1024]{1,0:T(8,128)(2,1)}, f32[3,32,128]{2,1,0:T(8,128)}, f32[4,1024]{1,0:T(4,128)}, f32[32,512]{1,0:T(8,128)}, /*index=5*/f32[16,1024]{1,0:T(8,128)}) custom-call(s32[12]{0:T(128)} %refs_0_.1, s32[12]{0:T(128)} %refs_1_.1, f32[1,1024]{1,0:T(1,128)} %bitcast.4, bf16[32,1024]{1,0:T(8,128)(2,1)} %refs_3_.1, ...), custom_call_target="tpu_custom_call" | custom-call | tf_op jit(solution)/shard_map/whole/pallas_call | solution.py:732
  107.9 1.9 %hand_over.1 = (bf16[128,1024]{1,0:T(8,128)(2,1)}, bf16[128,1024]{1,0:T(8,128)(2,1)}, f32[3,32,128]{2,1,0:T(8,128)}, f32[4,1024]{1,0:T(4,128)}, f32[32,512]{1,0:T(8,128)}, /*index=5*/f32[16,1024]{1,0:T(8,128)}) custom-call(bf16[128,1024]{1,0:T(8,128)(2,1)} %get-tuple-element.18.refs_0_, bf16[128,1024]{1,0:T(8,128)(2,1)} %get-tuple-element.19.refs_1_, ...), custom_call_target="tpu_custom_call" | custom-call | tf_op jit(solution)/shard_map/hand_over/pallas_call | solution.py:745

commit v6 on v5

--- a/solution.py
+++ b/solution.py
@@ -700,6 +700,8 @@
     wg["qkv"].spread()
     gin.turn(0)
     gin.turn(1)
+    layer_in()
+    layer_ref[...] = b.layer[...]
     gup_ref[...] = wg["up"].finish()
     total = wg["out"].finish()
     for q in range(4):
@@ -707,13 +709,11 @@
     total = wg["qkv"].finish()
     for c in range(3):
         gqkv_ref[c] = total[:, c * 128 : (c + 1) * 128]
+    for k, ref in pending:
+        wait(ss.at[k], ref)
     gin.finish()
     gtok_ref[...] = (b.grad_middle[...].astype(f32) + norm_back(
         b.tokens[...], b.gin_sum[...].astype(f32))).astype(bf16)
-    layer_in()
-    layer_ref[...] = b.layer[...]
-    for k, ref in pending:
-        wait(ss.at[k], ref)
 
 
 def hand_over(*refs):

time: 110 us -> 110 us (level)
  no operation moved by 1% of the time
where the time goes in v6:
time: 110 us
  Pallas kernels  109 us (99%)
    pallas_call x1, Pallas kernels, shards(): pl.pallas_call(whole_kernel, out_shape=[shape((ROWS, D), bf16), shape((RO...  107 us

profile of v6, /device:TPU:1, one launch (start us, length us, event | category | flops | bytes accessed | tf_op | source)
XLA Modules:
  0.0 109.6 jit_solution(6960649535426837929)
XLA Ops:
  0.6 107.0 %whole.1 = (bf16[128,1024]{1,0:T(8,128)(2,1)}, bf16[128,1024]{1,0:T(8,128)(2,1)}, f32[3,32,128]{2,1,0:T(8,128)}, f32[4,1024]{1,0:T(4,128)}, f32[32,512]{1,0:T(8,128)}, /*index=5*/f32[16,1024]{1,0:T(8,128)}) custom-call(s32[12]{0:T(128)} %refs_0_.1, s32[12]{0:T(128)} %refs_1_.1, f32[1,1024]{1,0:T(1,128)} %bitcast.4, bf16[32,1024]{1,0:T(8,128)(2,1)} %refs_3_.1, ...), custom_call_target="tpu_custom_call" | custom-call | tf_op jit(solution)/shard_map/whole/pallas_call | solution.py:732
  107.7 1.9 %hand_over.1 = (bf16[128,1024]{1,0:T(8,128)(2,1)}, bf16[128,1024]{1,0:T(8,128)(2,1)}, f32[3,32,128]{2,1,0:T(8,128)}, f32[4,1024]{1,0:T(4,128)}, f32[32,512]{1,0:T(8,128)}, /*index=5*/f32[16,1024]{1,0:T(8,128)}) custom-call(bf16[128,1024]{1,0:T(8,128)(2,1)} %get-tuple-element.18.refs_0_, bf16[128,1024]{1,0:T(8,128)(2,1)} %get-tuple-element.19.refs_1_, ...), custom_call_target="tpu_custom_call" | custom-call | tf_op jit(solution)/shard_map/hand_over/pallas_call | solution.py:745
